TPU v7x, 32 devices: a whole 2x2x4 slice. The times are simulated.
32 devices in a mesh: dp: 2 (over y), expert: 16 (over z, x, core).
Axes of the slice: x: 2, y: 2, z: 4, core: 2. Of those that a mesh axis runs over, the one named last changes fastest.
Arguments:
- tokens: bfloat16 [2048, 1024], P(('dp', 'expert')), may hold values from -6 to 6
- expert_ids: int32 [2048, 8], P(('dp', 'expert')), may hold values from 0 to 15, all different within a row; in each aligned block of 64 rows (0 to 63, 64 to 127, ...) at most 40 rows name the same one
- route_weight: float32 [2048, 8], P(('dp', 'expert')), may hold values from 0.05 to 0.5
- out_grad: bfloat16 [2048, 1024], P(('dp', 'expert')), may hold values from -6 to 6
- gate_weight: bfloat16 [16, 1024, 384], P('expert', 'dp'), may hold values from -0.1875 to 0.1875
- up_weight: bfloat16 [16, 1024, 384], P('expert', 'dp'), may hold values from -0.1875 to 0.1875
- down_weight: bfloat16 [16, 384, 1024], P('expert', None, 'dp'), may hold values from -0.3125 to 0.3125
Outputs:
- layer_out: bfloat16 [2048, 1024], P(('dp', 'expert'))
- token_grad: bfloat16 [2048, 1024], P(('dp', 'expert'))
- route_grad: float32 [2048, 8], P(('dp', 'expert'))
- gate_grad: float32 [16, 1024, 384], P('expert', 'dp')
- up_grad: float32 [16, 1024, 384], P('expert', 'dp')
- down_grad: float32 [16, 384, 1024], P('expert', None, 'dp')
Inputs may be any that keep to these rules, and one draw needn't show every extreme that they name: `expert_ids`: each token names 8 different experts. Among the 64 tokens of one device no expert is named by more than 40 tokens, and in every draw some expert is named by exactly 40 tokens of some device.
All inputs are finite; a program needn't handle non-finite values.
Results may differ from a plain program's by a relative error of at most 0.012.
Values may be sent and summed in bfloat16 or wider, within the bound.
A program may use at most 64 MiB of HBM per device.

v0:
```python
import jax
import jax.numpy as jnp
from jax import lax
from jax.sharding import PartitionSpec as P


def layout(live_counts, slot_cap, padded_rows):
    owners = live_counts.shape[0]
    ends = jnp.cumsum(live_counts).astype(jnp.int32)
    starts = ends - live_counts
    total = ends[owners - 1]
    positions = jnp.arange(padded_rows, dtype=jnp.int32)
    source = jnp.minimum(
        jnp.sum((positions[:, None] >= ends[None, :]).astype(jnp.int32), 1), owners - 1
    )
    matches = source[:, None] == jnp.arange(owners, dtype=jnp.int32)[None, :]
    offset = positions - jnp.sum(jnp.where(matches, starts[None, :], 0), 1)
    valid = positions < total
    pick_rows = jnp.where(valid, source * slot_cap + offset, 0)
    slot_pos = jnp.arange(owners * slot_cap, dtype=jnp.int32) % slot_cap
    live_back = slot_pos < jnp.repeat(live_counts, slot_cap)
    back_rows = jnp.where(live_back, jnp.repeat(starts, slot_cap) + slot_pos, 0)
    return (pick_rows, valid, back_rows, live_back, total)


def compact(received, pick_rows, valid):
    feat_width = received.shape[2]
    rows = received.reshape(-1, feat_width)[pick_rows]
    return jnp.where(valid[:, None], rows, jnp.zeros_like(rows))


def spread(rows, back_rows, live_back, owners, slot_cap):
    picked = rows[back_rows]
    picked = jnp.where(live_back[:, None], picked, jnp.zeros_like(picked))
    return picked.reshape(owners, slot_cap, rows.shape[1])


def shards(tokens, expert_ids, route_weight, out_grad, gate_weight, up_weight, down_weight):
    block_rows = 128
    tok_rows, feat_width = tokens.shape
    top_picks = expert_ids.shape[1]
    hidden_units = gate_weight.shape[2]
    owners = lax.axis_size("expert")
    slot_cap = max(2, 5 * tok_rows * top_picks // (4 * owners))
    slot_total = owners * slot_cap
    padded_rows = -(-slot_total // block_rows) * block_rows
    flat_ids = expert_ids.reshape(-1)
    one_hot = (flat_ids[:, None] == jnp.arange(owners, dtype=jnp.int32)[None, :]).astype(jnp.int32)
    slot_rank = jnp.sum((jnp.cumsum(one_hot, 0) - one_hot) * one_hot, 1)
    pair_slots = flat_ids * slot_cap + slot_rank
    send_counts = jnp.sum(one_hot, 0).reshape(owners, 1)
    x_send = (
        jnp.zeros((slot_total, feat_width), jnp.bfloat16)
        .at[pair_slots]
        .set(jnp.repeat(tokens, top_picks, 0))
        .reshape(owners, slot_cap, feat_width)
    )
    pair_grad = (
        route_weight.reshape(-1, 1) * jnp.repeat(out_grad, top_picks, 0).astype(jnp.float32)
    ).astype(jnp.bfloat16)
    dy_send = (
        jnp.zeros((slot_total, feat_width), jnp.bfloat16)
        .at[pair_slots]
        .set(pair_grad)
        .reshape(owners, slot_cap, feat_width)
    )
    gate_full, up_full, down_full = (
        lax.all_gather(gate_weight, "dp", axis=1, tiled=True),
        lax.all_gather(up_weight, "dp", axis=1, tiled=True),
        lax.all_gather(down_weight, "dp", axis=2, tiled=True),
    )
    gate_full = gate_full[0]
    up_full = up_full[0]
    down_full = down_full[0]
    x_recv, recv_counts = (
        lax.all_to_all(x_send, "expert", split_axis=0, concat_axis=0, tiled=True),
        lax.all_to_all(send_counts, "expert", split_axis=0, concat_axis=0, tiled=True),
    )
    pick_rows, valid, back_rows, live_back, total = layout(recv_counts[:, 0], slot_cap, padded_rows)
    live_blocks = (total + block_rows - 1) // block_rows
    x_rows = compact(x_recv, pick_rows, valid)

    def forward_block(block_id, carry):
        y_buf, h_buf, g_buf, u_buf = carry
        row_start = block_id * block_rows
        x_blk = lax.dynamic_slice_in_dim(x_rows, row_start, block_rows, 0)
        gate_act = jnp.dot(x_blk, gate_full, preferred_element_type=jnp.float32)
        up_act = jnp.dot(x_blk, up_full, preferred_element_type=jnp.float32)
        hidden = (gate_act * jax.nn.sigmoid(gate_act) * up_act).astype(jnp.bfloat16)
        y_blk = jnp.dot(hidden, down_full, preferred_element_type=jnp.float32).astype(jnp.bfloat16)
        return (
            lax.dynamic_update_slice_in_dim(y_buf, y_blk, row_start, 0),
            lax.dynamic_update_slice_in_dim(h_buf, hidden, row_start, 0),
            lax.dynamic_update_slice_in_dim(g_buf, gate_act, row_start, 0),
            lax.dynamic_update_slice_in_dim(u_buf, up_act, row_start, 0),
        )

    forward_init = (
        jnp.zeros((padded_rows, feat_width), jnp.bfloat16),
        jnp.zeros((padded_rows, hidden_units), jnp.bfloat16),
        jnp.zeros((padded_rows, hidden_units), jnp.float32),
        jnp.zeros((padded_rows, hidden_units), jnp.float32),
    )
    y_rows, h_rows, g_rows, u_rows = lax.fori_loop(0, live_blocks, forward_block, forward_init)
    y_back = lax.all_to_all(
        spread(y_rows, back_rows, live_back, owners, slot_cap),
        "expert",
        split_axis=0,
        concat_axis=0,
        tiled=True,
    )
    dy_recv = lax.all_to_all(dy_send, "expert", split_axis=0, concat_axis=0, tiled=True)
    dy_rows = compact(dy_recv, pick_rows, valid)
    contract_last = (((1,), (1,)), ((), ()))
    contract_rows = (((0,), (0,)), ((), ()))

    def backward_block(block_id, carry):
        dx_buf, act_buf = carry
        row_start = block_id * block_rows
        dy_blk = lax.dynamic_slice_in_dim(dy_rows, row_start, block_rows, 0)
        gate_act = lax.dynamic_slice_in_dim(g_rows, row_start, block_rows, 0)
        up_act = lax.dynamic_slice_in_dim(u_rows, row_start, block_rows, 0)
        sigmoid_g = jax.nn.sigmoid(gate_act)
        hidden_grad = lax.dot_general(
            dy_blk, down_full, contract_last, preferred_element_type=jnp.float32
        )
        gate_back = (
            hidden_grad * up_act * sigmoid_g * (1.0 + gate_act * (1.0 - sigmoid_g))
        ).astype(jnp.bfloat16)
        up_back = (hidden_grad * gate_act * sigmoid_g).astype(jnp.bfloat16)
        dx_blk = (
            lax.dot_general(gate_back, gate_full, contract_last, preferred_element_type=jnp.float32)
            + lax.dot_general(up_back, up_full, contract_last, preferred_element_type=jnp.float32)
        ).astype(jnp.bfloat16)
        act_back = jnp.concatenate([gate_back, up_back], 1)
        return (
            lax.dynamic_update_slice_in_dim(dx_buf, dx_blk, row_start, 0),
            lax.dynamic_update_slice_in_dim(act_buf, act_back, row_start, 0),
        )

    backward_init = (
        jnp.zeros((padded_rows, feat_width), jnp.bfloat16),
        jnp.zeros((padded_rows, 2 * hidden_units), jnp.bfloat16),
    )
    dx_rows, act_rows = lax.fori_loop(0, live_blocks, backward_block, backward_init)
    grad_total = jnp.concatenate(
        [
            lax.dot_general(x_rows, act_rows, contract_rows, preferred_element_type=jnp.float32),
            lax.dot_general(dy_rows, h_rows, contract_rows, preferred_element_type=jnp.float32),
        ],
        1,
    )
    dx_back = lax.all_to_all(
        spread(dx_rows, back_rows, live_back, owners, slot_cap),
        "expert",
        split_axis=0,
        concat_axis=0,
        tiled=True,
    )
    y_pairs = y_back.reshape(-1, feat_width)[pair_slots].reshape(tok_rows, top_picks, feat_width)
    dx_pairs = dx_back.reshape(-1, feat_width)[pair_slots].reshape(tok_rows, top_picks, feat_width)
    layer_out = jnp.sum(route_weight[:, :, None] * y_pairs.astype(jnp.float32), 1).astype(
        jnp.bfloat16
    )
    route_grad = jnp.einsum("td,tkd->tk", out_grad, y_pairs, preferred_element_type=jnp.float32)
    token_grad = jnp.sum(dx_pairs.astype(jnp.float32), 1).astype(jnp.bfloat16)
    local_rows = feat_width // lax.axis_size("dp")
    summed = lax.psum(grad_total.astype(jnp.bfloat16), "dp").astype(jnp.float32)
    mine = lax.dynamic_slice_in_dim(summed, lax.axis_index("dp") * local_rows, local_rows, 0)
    gate_grad = mine[:, :hidden_units][None]
    up_grad = mine[:, hidden_units : 2 * hidden_units][None]
    down_grad = mine[:, 2 * hidden_units :].T[None]
    return (layer_out, token_grad, route_grad, gate_grad, up_grad, down_grad)


def solution(mesh):
    placed = (
        P(("dp", "expert"), None),
        P(("dp", "expert"), None),
        P(("dp", "expert"), None),
        P(("dp", "expert"), None),
        P("expert", "dp", None),
        P("expert", "dp", None),
        P("expert", None, "dp"),
    )
    return jax.shard_map(
        shards,
        mesh=mesh,
        in_specs=placed,
        out_specs=(
            P(("dp", "expert"), None),
            P(("dp", "expert"), None),
            P(("dp", "expert"), None),
            P("expert", "dp", None),
            P("expert", "dp", None),
            P("expert", None, "dp"),
        ),
        check_vma=False,
    )
```

profile of v0, /device:TPU:0, one launch (start us, length us, event | category | flops | bytes accessed | tf_op | source)
XLA Modules:
  0.0 275.7 jit_solution(6795737027338271655)
XLA Ops:
  10.4 7.4 %all-to-all-start = ((s32[16,1,1]{2,1,0:T(1,128)}), s32[16,1,1]{2,1,0:T(1,128)S(1)}, u32[]{:S(2)}, u32[]{:S(2)}) async-start(s32[16,1,1]{2,1,0:T(1,128)} %copy.48), calls=%async_computation | async-start | bytes 16384 | tf_op jit(solution)/shard_map/all_to_all | solution.py:77
  21.1 3.8 %scatter_custom_fusion.1 = bf16[640,1024]{1,0:T(8,128)(2,1)} fusion(s32[512]{0:T(512)S(1)} %bitcast.95, f32[64,1024]{1,0:T(8,128)S(1)} %convert_element_type.52, f32[512]{0:T(512)S(1)} %mul.92, bf16[]{:T(256)} %constant.74.clone.1), kind=kCustom, calls=%fused_computation.41 | custom fusion | flops 1048576 | bytes 1574914 | tf_op jit(solution)/shard_map/scatter | solution.py:64
  24.9 6.0 %all-to-all-start.3 = ((bf16[16,40,1024]{2,1,0:T(8,128)(2,1)}), bf16[16,40,1024]{2,1,0:T(8,128)(2,1)S(1)}, u32[]{:S(2)}, u32[]{:S(2)}) async-start(bf16[16,40,1024]{2,1,0:T(8,128)(2,1)} %bitcast.16), calls=%async_computation.3 | async-start | bytes 2621440 | tf_op jit(solution)/shard_map/all_to_all | solution.py:112
  30.9 3.7 %scatter_custom_fusion = bf16[640,1024]{1,0:T(8,128)(2,1)} fusion(s32[512]{0:T(512)S(1)} %bitcast.96, bf16[]{:T(256)} %constant.74.clone.1, bf16[64,1024]{1,0:T(8,128)(2,1)S(1)} %copy-done), kind=kCustom, calls=%fused_computation.45 | custom fusion | bytes 1441794 | tf_op jit(solution)/shard_map/scatter | solution.py:55
  34.6 23.7 %all-to-all-done.3 = bf16[16,40,1024]{2,1,0:T(8,128)(2,1)S(1)} async-done(((bf16[16,40,1024]{2,1,0:T(8,128)(2,1)}), bf16[16,40,1024]{2,1,0:T(8,128)(2,1)S(1)}, u32[]{:S(2)}, u32[]{:S(2)}) %all-to-all-start.3) | async-done | bytes 1310752 | tf_op jit(solution)/shard_map/all_to_all | solution.py:112
  58.3 8.1 %all-to-all-start.1 = ((bf16[16,40,1024]{2,1,0:T(8,128)(2,1)}), bf16[16,40,1024]{2,1,0:T(8,128)(2,1)S(1)}, u32[]{:S(2)}, u32[]{:S(2)}) async-start(bf16[16,40,1024]{2,1,0:T(8,128)(2,1)} %bitcast.90), calls=%async_computation.1 | async-start | bytes 2621440 | tf_op jit(solution)/shard_map/all_to_all | solution.py:76
  66.5 12.4 %all_gather.10 = bf16[1,1024,384]{2,1,0:T(8,128)(2,1)} all-gather(bf16[1,512,384]{2,1,0:T(8,128)(2,1)S(1)} %copy-done.9), channel_id=1, replica_groups=mesh['dp'=2,'expert'=16] {'dp'}, dimensions={1}, use_global_device_ids=true | all-gather | bytes 1179648 | tf_op jit(solution)/shard_map/all_gather | solution.py:69
  78.9 11.4 %all_gather.11 = bf16[1,384,1024]{2,1,0:T(8,128)(2,1)} all-gather(bf16[1,384,512]{2,1,0:T(8,128)(2,1)S(1)} %copy-done.10), channel_id=1, replica_groups=mesh['dp'=2,'expert'=16] {'dp'}, dimensions={2}, use_global_device_ids=true | all-gather | bytes 1179648 | tf_op jit(solution)/shard_map/all_gather | solution.py:70
  90.3 10.4 %all_gather.9 = bf16[1,1024,384]{2,1,0:T(8,128)(2,1)S(1)} all-gather(bf16[1,512,384]{2,1,0:T(8,128)(2,1)S(1)} %copy-done.11), channel_id=1, replica_groups=mesh['dp'=2,'expert'=16] {'dp'}, dimensions={1}, use_global_device_ids=true | all-gather | bytes 1179648 | tf_op jit(solution)/shard_map/all_gather | solution.py:68
  108.6 3.5 %gather_fusion.3 = bf16[640,1024]{1,0:T(8,128)(2,1)} fusion(bf16[640,1024]{1,0:T(8,128)(2,1)S(1)} %bitcast.82, s32[1024]{0:T(1024)S(1)} %pad_clamp_fusion.2), kind=kCustom, calls=%fused_computation.3 | custom fusion | bytes 2624000 | tf_op jit(solution)/shard_map/gather | solution.py:28
  112.1 3.5 %gather_fusion = bf16[640,1024]{1,0:T(8,128)(2,1)} fusion(bf16[640,1024]{1,0:T(8,128)(2,1)S(1)} %bitcast.83, s32[1024]{0:T(1024)S(1)} %pad_clamp_fusion.2), kind=kCustom, calls=%fused_computation | custom fusion | bytes 2624000 | tf_op jit(solution)/shard_map/gather | solution.py:28
  115.6 3.1 %broadcast_select_fusion = (bf16[640,1024]{1,0:T(8,128)(2,1)}, bf16[640,1024]{1,0:T(8,128)(2,1)}) fusion(bf16[640,1024]{1,0:T(8,128)(2,1)S(1)} %copy-done.5, pred[640]{0:T(1024)(128)(4,1)S(1)} %copy-done.19, bf16[640,1024]{1,0:T(8,128)(2,1)} %gather_fusion), kind=kLoop, calls=%fused_computation.36 | loop fusion | flops 1310720 | bytes 5243520 | tf_op jit(solution)/shard_map/jit(_where)/select_n | solution.py:29
  120.9 21.5 %while.28 = (s32[]{:T(128)}, bf16[640,1024]{1,0:T(8,128)(2,1)S(1)}, bf16[640,384]{1,0:T(8,128)(2,1)S(1)}, f32[640,384]{1,0:T(8,128)}, f32[640,384]{1,0:T(8,128)}...) while((s32[]{:T(128)}, bf16[640,1024]{1,0:T(8,128)(2,1)S(1)}, ...), condition=%wide.region_9.10_spmd, body=%wide.region_8.9_spmd.sunk | while | flops 302415872 | bytes 7768279 | solution.py:104
  144.4 16.3 %while.29 = (s32[]{:T(128)}, bf16[640,1024]{1,0:T(8,128)(2,1)S(1)}, bf16[640,768]{1,0:T(8,128)(2,1)}, s32[]{:T(128)}, bf16[640,1024]{1,0:T(8,128)(2,1)}, /*index...) while((s32[]{:T(128)}, bf16[640,1024]{1,0:T(8,128)(2,1)S(1)}, ...), condition=%wide.region_13.14_spmd, body=%wide.region_12.13_spmd.sunk | while | flops 303284224 | bytes 8258775 | solution.py:145
  160.7 3.5 %gather_fusion.4 = bf16[640,1024]{1,0:T(8,128)(2,1)} fusion(bf16[640,1024]{1,0:T(8,128)(2,1)S(1)} %get-tuple-element.119, s32[1024]{0:T(1024)S(1)} %pad_clamp_fusion.1), kind=kCustom, calls=%fused_computation.4 | custom fusion | bytes 2624000 | tf_op jit(solution)/shard_map/gather | solution.py:33
  164.2 3.5 %gather_fusion.1 = bf16[640,1024]{1,0:T(8,128)(2,1)} fusion(bf16[640,1024]{1,0:T(8,128)(2,1)S(1)} %get-tuple-element.116, s32[1024]{0:T(1024)S(1)} %pad_clamp_fusion.1), kind=kCustom, calls=%fused_computation.1 | custom fusion | bytes 2624000 | tf_op jit(solution)/shard_map/gather | solution.py:33
  167.7 3.1 %broadcast_select_fusion.2 = (bf16[16,40,1024]{2,1,0:T(8,128)(2,1)}, bf16[16,40,1024]{2,1,0:T(8,128)(2,1)}) fusion(bf16[16,40,1024]{2,1,0:T(8,128)(2,1)S(1)} %bitcast.91, pred[16,40]{1,0:T(8,128)(4,1)S(1)} %fusion.28, bf16[16,40,1024]{2,1,0:T(8,128)(2,1)} %bitcast.92), kind=kLoop, calls=%fused_computation.38 | loop fusion | flops 1310720 | bytes 5243520 | tf_op jit(solution)/shard_map/jit(_where)/select_n | solution.py:34
  170.7 5.2 %all-to-all-start.4 = ((bf16[16,40,1024]{2,1,0:T(8,128)(2,1)}), bf16[16,40,1024]{2,1,0:T(8,128)(2,1)S(1)}, u32[]{:S(2)}, u32[]{:S(2)}) async-start(bf16[16,40,1024]{2,1,0:T(8,128)(2,1)} %get-tuple-element.206), calls=%async_computation.4 | async-start | bytes 2621440 | tf_op jit(solution)/shard_map/all_to_all | solution.py:153
  178.0 2.6 convolution_convert_fusion.1
  182.2 21.1 %all-to-all-done.4 = bf16[16,40,1024]{2,1,0:T(8,128)(2,1)S(1)} async-done(((bf16[16,40,1024]{2,1,0:T(8,128)(2,1)}), bf16[16,40,1024]{2,1,0:T(8,128)(2,1)S(1)}, u32[]{:S(2)}, u32[]{:S(2)}) %all-to-all-start.4) | async-done | bytes 1310752 | tf_op jit(solution)/shard_map/all_to_all | solution.py:153
  203.3 8.1 %all-to-all-start.2 = ((bf16[16,40,1024]{2,1,0:T(8,128)(2,1)}), bf16[16,40,1024]{2,1,0:T(8,128)(2,1)S(1)}, u32[]{:S(2)}, u32[]{:S(2)}) async-start(bf16[16,40,1024]{2,1,0:T(8,128)(2,1)} %get-tuple-element.207), calls=%async_computation.2 | async-start | bytes 2621440 | tf_op jit(solution)/shard_map/all_to_all | solution.py:105
  211.5 40.9 %all-reduce.2.cloned.1.call-done = bf16[1024,1152]{0,1:T(8,128)(2,1)} async-done(((bf16[1024,1152]{0,1:T(8,128)(2,1)}), bf16[1024,1152]{0,1:T(8,128)(2,1)}) %all-reduce.2.cloned.1.call-update) | async-done | bytes 2359312 | tf_op jit(solution)/shard_map/psum | solution.py:168
  258.7 2.8 %gather_fusion.5 = bf16[512,1024]{1,0:T(8,128)(2,1)} fusion(bf16[640,1024]{1,0:T(8,128)(2,1)S(1)} %bitcast.85, s32[1024]{0:T(1024)S(1)} %pad_clamp_fusion), kind=kCustom, calls=%fused_computation.5 | custom fusion | bytes 2099200 | tf_op jit(solution)/shard_map/gather | solution.py:161
  261.5 2.6 bitcast_reduce_fusion
  (153 shorter events, 70.1 us)
Async XLA Ops:
  7.2 23.7 %copy-start = (bf16[64,1024]{1,0:T(8,128)(2,1)S(1)}, bf16[64,1024]{1,0:T(8,128)(2,1)}, u32[]{:S(2)}) copy-start(bf16[64,1024]{1,0:T(8,128)(2,1)} %param.11) | copy-start | bytes 393220
  10.4 14.4 %all-to-all-start = ((s32[16,1,1]{2,1,0:T(1,128)}), s32[16,1,1]{2,1,0:T(1,128)S(1)}, u32[]{:S(2)}, u32[]{:S(2)}) async-start(s32[16,1,1]{2,1,0:T(1,128)} %copy.48), calls=%async_computation | async-start | bytes 16384 | tf_op jit(solution)/shard_map/all_to_all | solution.py:77
  21.1 9.8 %copy-start.15 = (s32[512,1]{0,1:T(1,128)}, s32[512,1]{0,1:T(1,128)S(1)}, u32[]{:S(2)}) copy-start(s32[512,1]{0,1:T(1,128)S(1)} %compare_select_fusion.2) | copy-start | bytes 6148
  24.9 33.4 %all-to-all-start.3 = ((bf16[16,40,1024]{2,1,0:T(8,128)(2,1)}), bf16[16,40,1024]{2,1,0:T(8,128)(2,1)S(1)}, u32[]{:S(2)}, u32[]{:S(2)}) async-start(bf16[16,40,1024]{2,1,0:T(8,128)(2,1)} %bitcast.16), calls=%async_computation.3 | async-start | bytes 2621440 | tf_op jit(solution)/shard_map/all_to_all | solution.py:112
  58.3 8.2 %copy-start.9 = (bf16[1,512,384]{2,1,0:T(8,128)(2,1)S(1)}, bf16[1,512,384]{2,1,0:T(8,128)(2,1)}, u32[]{:S(2)}) copy-start(bf16[1,512,384]{2,1,0:T(8,128)(2,1)} %param.16) | copy-start | bytes 1179652
  58.3 20.5 %copy-start.10 = (bf16[1,384,512]{2,1,0:T(8,128)(2,1)S(1)}, bf16[1,384,512]{2,1,0:T(8,128)(2,1)}, u32[]{:S(2)}) copy-start(bf16[1,384,512]{2,1,0:T(8,128)(2,1)} %param.17) | copy-start | bytes 1179652
  58.3 53.8 %all-to-all-start.1 = ((bf16[16,40,1024]{2,1,0:T(8,128)(2,1)}), bf16[16,40,1024]{2,1,0:T(8,128)(2,1)S(1)}, u32[]{:S(2)}, u32[]{:S(2)}) async-start(bf16[16,40,1024]{2,1,0:T(8,128)(2,1)} %bitcast.90), calls=%async_computation.1 | async-start | bytes 2621440 | tf_op jit(solution)/shard_map/all_to_all | solution.py:76
  66.5 23.8 %copy-start.11 = (bf16[1,512,384]{2,1,0:T(8,128)(2,1)S(1)}, bf16[1,512,384]{2,1,0:T(8,128)(2,1)}, u32[]{:S(2)}) copy-start(bf16[1,512,384]{2,1,0:T(8,128)(2,1)} %param.15) | copy-start | bytes 1179652
  112.1 3.5 %copy-start.5 = (bf16[640,1024]{1,0:T(8,128)(2,1)S(1)}, bf16[640,1024]{1,0:T(8,128)(2,1)}, u32[]{:S(2)}) copy-start(bf16[640,1024]{1,0:T(8,128)(2,1)} %gather_fusion.3) | copy-start | bytes 3932164
  112.1 3.5 %copy-start.19 = (pred[640]{0:T(1024)(128)(4,1)S(1)}, pred[640]{0:T(1024)(128)(4,1)}, u32[]{:S(2)}) copy-start(pred[640]{0:T(1024)(128)(4,1)} %iota_compare_fusion.4) | copy-start | bytes 1924
  121.0 3.3 %copy-start.3 = (bf16[384,1024]{1,0:T(8,128)(2,1)S(1)}, bf16[384,1024]{1,0:T(8,128)(2,1)}, u32[]{:S(2)}) copy-start(bf16[384,1024]{1,0:T(8,128)(2,1)} %get-tuple-element.385) | copy-start | bytes 2359300 | tf_op jit(solution)/shard_map/while
  125.3 3.3 %copy-start.3 = (bf16[384,1024]{1,0:T(8,128)(2,1)S(1)}, bf16[384,1024]{1,0:T(8,128)(2,1)}, u32[]{:S(2)}) copy-start(bf16[384,1024]{1,0:T(8,128)(2,1)} %get-tuple-element.385) | copy-start | bytes 2359300 | tf_op jit(solution)/shard_map/while
  129.5 3.3 %copy-start.3 = (bf16[384,1024]{1,0:T(8,128)(2,1)S(1)}, bf16[384,1024]{1,0:T(8,128)(2,1)}, u32[]{:S(2)}) copy-start(bf16[384,1024]{1,0:T(8,128)(2,1)} %get-tuple-element.385) | copy-start | bytes 2359300 | tf_op jit(solution)/shard_map/while
  133.8 3.3 %copy-start.3 = (bf16[384,1024]{1,0:T(8,128)(2,1)S(1)}, bf16[384,1024]{1,0:T(8,128)(2,1)}, u32[]{:S(2)}) copy-start(bf16[384,1024]{1,0:T(8,128)(2,1)} %get-tuple-element.385) | copy-start | bytes 2359300 | tf_op jit(solution)/shard_map/while
  138.1 3.3 %copy-start.3 = (bf16[384,1024]{1,0:T(8,128)(2,1)S(1)}, bf16[384,1024]{1,0:T(8,128)(2,1)}, u32[]{:S(2)}) copy-start(bf16[384,1024]{1,0:T(8,128)(2,1)} %get-tuple-element.385) | copy-start | bytes 2359300 | tf_op jit(solution)/shard_map/while
  144.4 2.2 copy-start.2
  150.9 2.2 copy-start.2
  164.2 3.5 %copy-start.6 = (bf16[640,1024]{1,0:T(8,128)(2,1)S(1)}, bf16[640,1024]{1,0:T(8,128)(2,1)}, u32[]{:S(2)}) copy-start(bf16[640,1024]{1,0:T(8,128)(2,1)} %gather_fusion.4) | copy-start | bytes 3932164
  170.7 5.2 %copy-start.7 = (bf16[640,1024]{1,0:T(8,128)(2,1)S(1)}, bf16[640,1024]{1,0:T(8,128)(2,1)}, u32[]{:S(2)}) copy-start(bf16[640,1024]{1,0:T(8,128)(2,1)} %get-tuple-element.447) | copy-start | bytes 3932164
  170.7 32.6 %all-to-all-start.4 = ((bf16[16,40,1024]{2,1,0:T(8,128)(2,1)}), bf16[16,40,1024]{2,1,0:T(8,128)(2,1)S(1)}, u32[]{:S(2)}, u32[]{:S(2)}) async-start(bf16[16,40,1024]{2,1,0:T(8,128)(2,1)} %get-tuple-element.206), calls=%async_computation.4 | async-start | bytes 2621440 | tf_op jit(solution)/shard_map/all_to_all | solution.py:153
  175.9 76.4 %all-reduce.2.cloned.1.call-start = ((), (), s32[]{:S(2)}) async-start(), calls=%async_computation.5 | async-start | bytes 4718592 | tf_op jit(solution)/shard_map/psum | solution.py:168
  203.3 8.2 %copy-start.16 = (s32[512,1]{0,1:T(1,128)S(1)}, s32[512,1]{0,1:T(1,128)}, u32[]{:S(2)}) copy-start(s32[512,1]{0,1:T(1,128)} %copy-done.15) | copy-start | bytes 6148
  203.3 60.8 %all-to-all-start.2 = ((bf16[16,40,1024]{2,1,0:T(8,128)(2,1)}), bf16[16,40,1024]{2,1,0:T(8,128)(2,1)S(1)}, u32[]{:S(2)}, u32[]{:S(2)}) async-start(bf16[16,40,1024]{2,1,0:T(8,128)(2,1)} %get-tuple-element.207), calls=%async_computation.2 | async-start | bytes 2621440 | tf_op jit(solution)/shard_map/all_to_all | solution.py:105
  264.1 3.4 %copy-start.14 = (bf16[64,1024]{1,0:T(8,128)(2,1)S(1)}, bf16[64,1024]{1,0:T(8,128)(2,1)}, u32[]{:S(2)}) copy-start(bf16[64,1024]{1,0:T(8,128)(2,1)} %param.14) | copy-start | bytes 393220
  (10 other events, 15.9 us)
Sparse Core Ops, SparseCore 0:
  182.3 69.9 all-reduce.1
where the time goes:
time: 277 us; the launch traced here: 276 us
  waiting for transfers between devices  85.7 us (31%)
  local copies, waits for them, and re-layouts  40.6 us (15%)
  matrix products  35.8 us (13%)
  starting transfers between devices  34.9 us (13%)
  blocking collectives  34.2 us (12%)
  other arithmetic  29.3 us (11%)
  between operations  15 us (5%)
    psum x1, waiting for transfers between devices, shards(): summed = lax.psum(grad_total.astype(jnp.bfloat16), 'dp').astype(jnp.float32)  40.9 us
    all_to_all x1, waiting for transfers between devices, shards(): lax.all_to_all(dy_send, 'expert', split_axis=0, concat_axis=0, tiled=True)  23.7 us
    all_to_all x1, waiting for transfers between devices, shards(): lax.all_to_all(spread(dx_rows, back_rows, live_back, owners, slot_cap), '...  21.1 us
    all_gather x1, blocking collectives, shards(): lax.all_gather(up_weight, 'dp', axis=1, tiled=True)  12.4 us
    all_gather x1, blocking collectives, shards(): lax.all_gather(down_weight, 'dp', axis=2, tiled=True)  11.4 us
    all_gather x1, blocking collectives, shards(): lax.all_gather(gate_weight, 'dp', axis=1, tiled=True)  10.4 us
    dot_general x5, matrix products, forward_block(): gate_act = jnp.dot(x_blk, gate_full, preferred_element_type=jnp.float32)  10 us
    dot_general x5, matrix products, backward_block(): lax.dot_general(dy_blk, down_full, contract_last, preferred_element_type=...  8.82 us
  transfers between devices with their start and end apart: 6, of which 3 were waited for; matrix products, arithmetic and copies ran while one was open for 14% of the time, Pallas kernels for 0%

commit v1 on v0

v1 whole, which is shorter than its diff:
```python
import functools

import jax
import jax.numpy as jnp
from jax import lax
from jax.experimental import pallas as pl
from jax.experimental.pallas import tpu as pltpu
from jax.sharding import PartitionSpec as P

MESH = pl.DeviceIdType.MESH
LANES = 128
HALF = 64
F32 = jnp.float32
BF16 = jnp.bfloat16
LAST = (((1,), (1,)), ((), ()))
ROWS = (((0,), (0,)), ((), ()))


def kernel(
    n, m,
    tok, ids, rw, og, gw, uw, dw,
    lo_ref, tg_ref, rg_ref, gg, ug, dg,
    pay, gu, dn, gb, hw, crecv, xrecv, zrecv, gstage, grecv, dstage, drecv,
    brecv_s, usend_s, dsend_s, xsend_s, csend_s, wsend_s, wrecv_s,
    gsend_s, grecv_s, qsend_s, qrecv_s,
    c2send_s, c2recv_s, x2send_s, x2recv_s, z2send_s, z2recv_s,
):
    tb, d_all = tok.shape
    dl, hid = gw.shape[1], gw.shape[2]
    top = ids.shape[1]
    nz = n // 4
    chunk = 4 * tb
    total = n * tb
    me = lax.axis_index("expert")
    dp = lax.axis_index("dp")
    c = me % 2
    x = (me // 2) % 2
    z = me // 4
    xp = me + 2 - 4 * x
    cp = me + 1 - 2 * c

    def rows(b):
        return pl.ds(pl.multiple_of(b * tb, tb), tb)

    def span(d):
        return pl.ds(pl.multiple_of(d * chunk, chunk), chunk)

    def block(zz, xx, cc):
        return zz * 4 + xx * 2 + cc

    def remote(src, dst, send, recv, **where):
        return pltpu.make_async_remote_copy(
            src_ref=src, dst_ref=dst, send_sem=send, recv_sem=recv,
            device_id=where, device_id_type=MESH,
        )

    lane = lax.broadcasted_iota(jnp.int32, (tb, LANES), 1)
    lane_mod = jnp.where(lane < HALF, lane, lane - HALF)
    dense = jnp.zeros((tb, LANES), F32)
    for k in range(top):
        dense = dense + jnp.where(ids[:, k : k + 1] == lane_mod, rw[:, k : k + 1], 0.0)
    hi = dense.astype(BF16).astype(F32)
    pay[rows(me), 0:d_all] = tok[...]
    pay[rows(me), d_all : 2 * d_all] = og[...]
    pay[rows(me), 2 * d_all :] = jnp.where(lane < HALF, hi, dense - hi).astype(BF16)

    barrier = pltpu.get_barrier_semaphore()
    for partner in (xp, cp):
        pl.semaphore_signal(barrier, inc=1, device_id={"expert": partner}, device_id_type=MESH)

    @pl.when(z > 0)
    def _():
        pl.semaphore_signal(barrier, inc=1, device_id={"expert": me - 4}, device_id_type=MESH)

    @pl.when(z < nz - 1)
    def _():
        pl.semaphore_signal(barrier, inc=1, device_id={"expert": me + 4}, device_id_type=MESH)

    for j in range(1, m):
        pl.semaphore_signal(barrier, inc=1, device_id={"dp": (dp + j) % m}, device_id_type=MESH)
    lines = jnp.minimum(z, 1) + jnp.minimum(nz - 1 - z, 1)
    pl.semaphore_wait(barrier, 1 + m + lines)

    my_rows = pl.ds(pl.multiple_of(dp * dl, dl), dl)

    def weight_copies(peer, owner):
        own = pl.ds(pl.multiple_of(owner * dl, dl), dl)
        return (
            remote(gw.at[0], gu.at[own, 0:hid], wsend_s.at[peer, 0], wrecv_s.at[owner, 0], dp=peer),
            remote(uw.at[0], gu.at[own, hid:], wsend_s.at[peer, 1], wrecv_s.at[owner, 1], dp=peer),
            remote(dw.at[0], dn.at[:, own], wsend_s.at[peer, 2], wrecv_s.at[owner, 2], dp=peer),
        )

    for j in range(1, m):
        for copy in weight_copies((dp + j) % m, dp):
            copy.start()

    def gather_copy(b, sem, to):
        return remote(pay.at[rows(b)], pay.at[rows(b)], sem, brecv_s.at[b], expert=to)

    def up(zz):
        return gather_copy(block(zz, x, c), usend_s.at[zz], me + 4)

    def down(zz):
        return gather_copy(block(zz, x, c), dsend_s.at[zz], me - 4)

    def across(zz):
        return gather_copy(block(zz, x, c), xsend_s.at[zz], xp)

    def core(zz, xx):
        return gather_copy(block(zz, xx, c), csend_s.at[zz * 2 + xx], cp)

    def arrived(b):
        gather_copy(b, xsend_s.at[0], xp).wait_recv()

    @pl.when(z < nz - 1)
    def _():
        up(z).start()

    @pl.when(z > 0)
    def _():
        down(z).start()

    across(z).start()
    core(z, x).start()
    gu[my_rows, 0:hid] = gw[0]
    gu[my_rows, hid:] = uw[0]
    dn[:, my_rows] = dw[0]

    def partner_blocks(s):
        @pl.when(s == 0)
        def _():
            arrived(block(z, 1 - x, c))
            core(z, 1 - x).start()

        @pl.when((s > 0) & (z - s >= 0))
        def _():
            arrived(block(z - s, 1 - x, c))
            core(z - s, 1 - x).start()

        @pl.when((s > 0) & (z + s < nz))
        def _():
            arrived(block(z + s, 1 - x, c))
            core(z + s, 1 - x).start()

    def gather_step(s, carry):
        @pl.when(z - s >= 0)
        def _():
            arrived(block(z - s, x, c))

            @pl.when(z < nz - 1)
            def _():
                up(z - s).start()

            across(z - s).start()
            core(z - s, x).start()

        @pl.when(z + s < nz)
        def _():
            arrived(block(z + s, x, c))

            @pl.when(z > 0)
            def _():
                down(z + s).start()

            across(z + s).start()
            core(z + s, x).start()

        partner_blocks(s - 1)
        return carry

    lax.fori_loop(1, nz, gather_step, 0)
    partner_blocks(nz - 1)

    def gather_end(zz, carry):
        arrived(block(zz, 0, 1 - c))
        arrived(block(zz, 1, 1 - c))

        @pl.when((z < nz - 1) & (zz <= z))
        def _():
            up(zz).wait_send()

        @pl.when((z > 0) & (zz >= z))
        def _():
            down(zz).wait_send()

        across(zz).wait_send()
        core(zz, 0).wait_send()
        core(zz, 1).wait_send()
        return carry

    lax.fori_loop(0, nz, gather_end, 0)
    for j in range(1, m):
        other = (dp + j) % m
        for copy in weight_copies(other, other):
            copy.wait_recv()

    wide = lax.broadcasted_iota(jnp.int32, (chunk, LANES), 1)
    mine_hi = wide == me
    mine_lo = wide == me + HALF

    def act_step(r, carry):
        act = jnp.dot(pay[span(r), 0:d_all], gu[...], preferred_element_type=F32)
        raw = lax.dot_general(pay[span(r), d_all : 2 * d_all], dn[...], LAST, preferred_element_type=F32)
        weights = pay[span(r), 2 * d_all :].astype(F32)
        w = jnp.sum(jnp.where(mine_hi | mine_lo, weights, 0.0), 1, keepdims=True)
        gate_act, up_act = act[:, 0:hid], act[:, hid:]
        sig = jax.nn.sigmoid(gate_act)
        silu = gate_act * sig
        hidden = silu * up_act
        hw[span(r), :] = (w * hidden).astype(BF16)
        route = jnp.sum(hidden * raw, 1, keepdims=True)
        route_hi = route.astype(BF16).astype(F32)
        pay[span(r), 2 * d_all :] = jnp.where(
            mine_hi, route_hi, jnp.where(mine_lo, route - route_hi, 0.0)
        ).astype(BF16)
        back = w * raw
        gb[span(r), 0:hid] = (back * up_act * sig * (1.0 + gate_act * (1.0 - sig))).astype(BF16)
        gb[span(r), hid:] = (back * silu).astype(BF16)
        return carry

    lax.fori_loop(0, nz, act_step, 0)

    piece = min(256, dl)
    pieces = dl // piece
    depth = min(total, 1024)

    def contract(left, right):
        def part(i):
            at = pl.ds(i * depth, depth) if isinstance(i, int) else pl.ds(pl.multiple_of(i * depth, depth), depth)
            return lax.dot_general(left(at), right(at), ROWS, preferred_element_type=F32)

        if total == depth:
            return part(0)
        return lax.fori_loop(1, total // depth, lambda i, acc: acc + part(i), part(0))

    def features(owner, i, shift):
        return pl.ds(pl.multiple_of(shift + owner * dl + i * piece, piece), piece)

    def gate_part(owner, i):
        return contract(lambda at: pay[at, features(owner, i, 0)], lambda at: gb[at, :])

    def down_part(owner, i):
        return contract(lambda at: hw[at, :], lambda at: pay[at, features(owner, i, d_all)])

    def cut(i):
        return pl.ds(pl.multiple_of(i * piece, piece), piece)

    def gate_copy(peer, owner, i):
        return remote(
            gstage.at[peer, cut(i)], grecv.at[owner, cut(i)],
            gsend_s.at[peer, i], grecv_s.at[owner, i], dp=peer,
        )

    def down_copy(peer, owner, i):
        return remote(
            dstage.at[peer, i], drecv.at[owner, i], qsend_s.at[peer, i], qrecv_s.at[owner, i], dp=peer
        )

    def share_step(t, carry):
        peer = (dp + 1 + t // pieces) % m
        i = t % pieces
        dstage[peer, i] = down_part(peer, i).astype(BF16)
        down_copy(peer, dp, i).start()
        gstage[peer, cut(i)] = gate_part(peer, i).astype(BF16)
        gate_copy(peer, dp, i).start()
        return carry

    lax.fori_loop(0, (m - 1) * pieces, share_step, 0)

    def own_step(i, carry):
        dg[0, :, cut(i)] = down_part(dp, i)
        own = gate_part(dp, i)
        gg[0, cut(i), :] = own[:, 0:hid]
        ug[0, cut(i), :] = own[:, hid:]
        return carry

    lax.fori_loop(0, pieces, own_step, 0)

    def order(p):
        odd = p % 2
        return (p // 2) * (1 - odd) + (nz - 1 - p // 2) * odd

    def core_back(d, xx):
        return remote(
            pay.at[rows(block(d, xx, 1 - c))], crecv.at[d * 2 + xx],
            c2send_s.at[d * 2 + xx], c2recv_s.at[d * 2 + xx], expert=cp,
        )

    def across_back(d):
        return remote(pay.at[rows(block(d, 1 - x, c))], xrecv.at[d], x2send_s.at[d], x2recv_s.at[d], expert=xp)

    def line_back(d, slot, to):
        return remote(pay.at[rows(block(d, x, c))], zrecv.at[slot], z2send_s.at[d], z2recv_s.at[slot], expert=to)

    def add(b, got):
        pay[rows(b), :] = (pay[rows(b), :].astype(F32) + got[...].astype(F32)).astype(BF16)

    def out_step(p, carry):
        d = order(p)
        pay[span(d), 0:d_all] = jnp.dot(hw[span(d), :], dn[...], preferred_element_type=F32).astype(BF16)
        pay[span(d), d_all : 2 * d_all] = lax.dot_general(
            gb[span(d), :], gu[...], LAST, preferred_element_type=F32
        ).astype(BF16)
        core_back(d, 0).start()
        core_back(d, 1).start()
        return carry

    lax.fori_loop(0, nz, out_step, 0)

    def across_step(p, carry):
        d = order(p)
        core_back(d, 0).wait_recv()
        core_back(d, 1).wait_recv()
        add(block(d, 0, c), crecv.at[d * 2])
        add(block(d, 1, c), crecv.at[d * 2 + 1])
        across_back(d).start()
        return carry

    lax.fori_loop(0, nz, across_step, 0)

    def take_line(d, slot):
        line_back(d, slot, xp).wait_recv()
        add(block(d, x, c), zrecv.at[slot])

    def line_step(p, carry):
        d = order(p)
        across_back(d).wait_recv()
        add(block(d, x, c), xrecv.at[d])

        @pl.when(d < z)
        def _():
            @pl.when(z < nz - 1)
            def _():
                take_line(d, d)

            line_back(d, d, me - 4).start()

        @pl.when(d > z)
        def _():
            @pl.when(z > 0)
            def _():
                take_line(d, d)

            @pl.when(d > z + 1)
            def _():
                line_back(d, d, me + 4).start()

            @pl.when(d == z + 1)
            def _():
                line_back(d, nz, me + 4).start()

        return carry

    lax.fori_loop(0, nz, line_step, 0)

    @pl.when(z < nz - 1)
    def _():
        take_line(z, z)

    @pl.when(z > 0)
    def _():
        take_line(z, nz)

    lo_ref[...] = pay[rows(me), 0:d_all]
    tg_ref[...] = pay[rows(me), d_all : 2 * d_all]
    route = pay[rows(me), 2 * d_all :].astype(F32)
    slot = lax.broadcasted_iota(jnp.int32, (tb, top), 1)
    picked = jnp.zeros((tb, top), F32)
    for k in range(top):
        value = jnp.sum(jnp.where(ids[:, k : k + 1] == lane_mod, route, 0.0), 1, keepdims=True)
        picked = jnp.where(slot == k, value, picked)
    rg_ref[...] = picked

    def share_end(t, carry):
        peer = (dp + 1 + t // pieces) % m
        i = t % pieces
        down_copy(peer, peer, i).wait()
        gate_copy(peer, peer, i).wait()
        dg[0, :, cut(i)] += drecv[peer, i].astype(F32)
        gg[0, cut(i), :] += grecv[peer, cut(i), 0:hid].astype(F32)
        ug[0, cut(i), :] += grecv[peer, cut(i), hid:].astype(F32)
        return carry

    lax.fori_loop(0, (m - 1) * pieces, share_end, 0)

    for j in range(1, m):
        for copy in weight_copies((dp + j) % m, dp):
            copy.wait_send()

    def sends_end(d, carry):
        core_back(d, 0).wait_send()
        core_back(d, 1).wait_send()
        across_back(d).wait_send()

        @pl.when(d != z)
        def _():
            line_back(d, d, xp).wait_send()

        return carry

    lax.fori_loop(0, nz, sends_end, 0)


def shards(tokens, expert_ids, route_weight, out_grad, gate_weight, up_weight, down_weight):
    tb, d_all = tokens.shape
    dl, hid = gate_weight.shape[1:]
    n, m = lax.axis_size("expert"), lax.axis_size("dp")
    nz = n // 4
    total = n * tb
    width = 2 * d_all + LANES
    piece = min(256, dl)
    pieces = dl // piece
    dma = pltpu.SemaphoreType.DMA
    vmem = pl.BlockSpec(memory_space=pltpu.VMEM)
    return tuple(
        pl.pallas_call(
            functools.partial(kernel, n, m),
            out_shape=(
                jax.ShapeDtypeStruct((tb, d_all), BF16),
                jax.ShapeDtypeStruct((tb, d_all), BF16),
                jax.ShapeDtypeStruct(expert_ids.shape, F32),
                jax.ShapeDtypeStruct((1, dl, hid), F32),
                jax.ShapeDtypeStruct((1, dl, hid), F32),
                jax.ShapeDtypeStruct((1, hid, dl), F32),
            ),
            in_specs=[vmem] * 7,
            out_specs=tuple([vmem] * 6),
            scratch_shapes=[
                pltpu.VMEM((total, width), BF16),
                pltpu.VMEM((d_all, 2 * hid), BF16),
                pltpu.VMEM((hid, d_all), BF16),
                pltpu.VMEM((total, 2 * hid), BF16),
                pltpu.VMEM((total, hid), BF16),
                pltpu.VMEM((2 * nz, tb, width), BF16),
                pltpu.VMEM((nz, tb, width), BF16),
                pltpu.VMEM((nz + 1, tb, width), BF16),
                pltpu.VMEM((m, dl, 2 * hid), BF16),
                pltpu.VMEM((m, dl, 2 * hid), BF16),
                pltpu.VMEM((m, pieces, hid, piece), BF16),
                pltpu.VMEM((m, pieces, hid, piece), BF16),
                dma((n,)), dma((nz,)), dma((nz,)), dma((nz,)), dma((2 * nz,)), dma((m, 3)), dma((m, 3)),
                dma((m, pieces)), dma((m, pieces)), dma((m, pieces)), dma((m, pieces)),
                dma((2 * nz,)), dma((2 * nz,)), dma((nz,)), dma((nz,)), dma((nz,)), dma((nz + 1,)),
            ],
            compiler_params=pltpu.CompilerParams(
                collective_id=0, has_side_effects=True, vmem_limit_bytes=60 * 1024 * 1024
            ),
        )(tokens, expert_ids, route_weight, out_grad, gate_weight, up_weight, down_weight)
    )


def solution(mesh):
    rows = P(("dp", "expert"), None)
    return jax.shard_map(
        shards,
        mesh=mesh,
        in_specs=(rows, rows, rows, rows, P("expert", "dp", None), P("expert", "dp", None), P("expert", None, "dp")),
        out_specs=(rows, rows, rows, P("expert", "dp", None), P("expert", "dp", None), P("expert", None, "dp")),
        check_vma=False,
    )
```

time: 277 us -> 99.2 us (0.36)
  the two profiles are of different devices: /device:TPU:0 before, /device:TPU:22 now
where the time goes in v1:
time: 99.2 us; the launch traced here: 98.8 us
  Pallas kernels  88 us (89%)
  local copies, waits for them, and re-layouts  10.2 us (10%)
    pallas_call x1, Pallas kernels, shards(): pl.pallas_call(functools.partial(kernel, n, m), out_shape=(jax.ShapeDtype...  88 us
    unnamed x15, local copies, waits for them, and re-layouts  8.79 us

profile of v1, /device:TPU:22, one launch (start us, length us, event | category | flops | bytes accessed | tf_op | source)
XLA Modules:
  0.0 98.8 jit_solution(4840219336129029458)
XLA Ops:
  0.6 0.0 copy-start.3
  0.6 1.4 %copy.13.ids = s32[64,8]{1,0:T(8,128)} copy(s32[64,8]{0,1:T(8,128)} %param.8) | data formatting | bytes 4096 | tf_op args[1]
  2.0 0.0 copy-done.3
  2.0 0.7 copy.14.rw
  2.7 88.0 %shard_map.118 = (bf16[64,1024]{1,0:T(8,128)(2,1)}, bf16[64,1024]{1,0:T(8,128)(2,1)}, f32[64,8]{1,0:T(8,128)}, f32[1,512,384]{2,1,0:T(8,128)}, f32[1,512,384]{2,1,0:T(8,128)}, /*index=5*/f32[1,384,512]{2,1,0:T(8,128)}) custom-call(bf16[64,1024]{1,0:T(8,128)(2,1)} %tok.1, s32[64,8]{1,0:T(8,128)} %copy.13.ids, f32[64,8]{1,0:T(8,128)} %copy.14.rw, ...), custom_call_target="tpu_custom_call" | custom-call | tf_op jit(solution)/shard_map/pallas_call | solution.py:417
  90.7 1.4 %copy.15 = f32[64,8]{0,1:T(8,128)} copy(f32[64,8]{1,0:T(8,128)} %get-tuple-element.8) | data formatting | bytes 4096 | tf_op jit(solution)/shard_map/pallas_call | solution.py:417
  92.1 0.0 copy-start.2
  92.1 1.6 %copy.21 = bf16[64,1024]{1,0:T(8,128)(2,1)} copy(bf16[64,1024]{1,0:T(8,128)(2,1)} %get-tuple-element.18) | data formatting | bytes 262144
  93.7 0.0 copy-done.2
  93.7 0.7 copy.22
  94.4 0.0 copy-start.1
  94.4 2.1 %copy.23 = f32[1,512,384]{2,1,0:T(8,128)} copy(f32[1,512,384]{2,1,0:T(8,128)} %get-tuple-element.21) | data formatting | bytes 1572864
  96.5 0.0 copy-done.1
  96.5 0.0 copy-start
  96.5 0.9 copy.24
  97.4 0.5 copy-done
  97.9 0.9 copy.25
Async XLA Ops:
  0.6 1.4 %copy-start.3 = (f32[64,8]{0,1:T(8,128)S(1)}, f32[64,8]{0,1:T(8,128)}, u32[]{:S(2)}) copy-start(f32[64,8]{0,1:T(8,128)} %param.9) | copy-start | bytes 6148
  92.1 1.6 %copy-start.2 = (bf16[64,1024]{1,0:T(8,128)(2,1)S(1)}, bf16[64,1024]{1,0:T(8,128)(2,1)}, u32[]{:S(2)}) copy-start(bf16[64,1024]{1,0:T(8,128)(2,1)} %get-tuple-element.19) | copy-start | bytes 393220
  94.4 2.1 %copy-start.1 = (f32[1,512,384]{2,1,0:T(8,128)S(1)}, f32[1,512,384]{2,1,0:T(8,128)}, u32[]{:S(2)}) copy-start(f32[1,512,384]{2,1,0:T(8,128)} %get-tuple-element.22) | copy-start | bytes 2359300
  96.5 1.4 %copy-start = (f32[1,384,512]{2,1,0:T(8,128)S(1)}, f32[1,384,512]{2,1,0:T(8,128)}, u32[]{:S(2)}) copy-start(f32[1,384,512]{2,1,0:T(8,128)} %get-tuple-element.23) | copy-start | bytes 2359300

commit v2 on v1

--- a/solution.py
+++ b/solution.py
@@ -17,17 +17,19 @@
 
 
 def kernel(
-    n, m,
-    tok, ids, rw, og, gw, uw, dw,
+    n, m, split,
+    tok, ids_t, rw_t, og, gw, uw, dw,
     lo_ref, tg_ref, rg_ref, gg, ug, dg,
-    pay, gu, dn, gb, hw, crecv, xrecv, zrecv, gstage, grecv, dstage, drecv,
+    pay, gu, dn, gb, hw, hh, crecv, xrecv, zrecv, gstage, grecv, dstage, drecv,
     brecv_s, usend_s, dsend_s, xsend_s, csend_s, wsend_s, wrecv_s,
     gsend_s, grecv_s, qsend_s, qrecv_s,
     c2send_s, c2recv_s, x2send_s, x2recv_s, z2send_s, z2recv_s,
+    *sums,
 ):
     tb, d_all = tok.shape
     dl, hid = gw.shape[1], gw.shape[2]
-    top = ids.shape[1]
+    top = ids_t.shape[0]
+    yb = sums[0] if split else pay
     nz = n // 4
     chunk = 4 * tb
     total = n * tb
@@ -54,6 +56,8 @@
             device_id=where, device_id_type=MESH,
         )
 
+    ids = ids_t[...].T
+    rw = rw_t[...].T
     lane = lax.broadcasted_iota(jnp.int32, (tb, LANES), 1)
     lane_mod = jnp.where(lane < HALF, lane, lane - HALF)
     dense = jnp.zeros((tb, LANES), F32)
@@ -83,16 +87,19 @@
 
     my_rows = pl.ds(pl.multiple_of(dp * dl, dl), dl)
 
-    def weight_copies(peer, owner):
+    def weight_copies(peer, owner, which=(0, 1, 2)):
         own = pl.ds(pl.multiple_of(owner * dl, dl), dl)
-        return (
-            remote(gw.at[0], gu.at[own, 0:hid], wsend_s.at[peer, 0], wrecv_s.at[owner, 0], dp=peer),
-            remote(uw.at[0], gu.at[own, hid:], wsend_s.at[peer, 1], wrecv_s.at[owner, 1], dp=peer),
-            remote(dw.at[0], dn.at[:, own], wsend_s.at[peer, 2], wrecv_s.at[owner, 2], dp=peer),
+        ends = (
+            (gw.at[0], gu.at[own, 0:hid]),
+            (uw.at[0], gu.at[own, hid:]),
+            (dw.at[0], dn.at[:, own]),
         )
+        return [
+            remote(*ends[i], wsend_s.at[peer, i], wrecv_s.at[owner, i], dp=peer) for i in which
+        ]
 
     for j in range(1, m):
-        for copy in weight_copies((dp + j) % m, dp):
+        for copy in weight_copies((dp + j) % m, dp, (0, 1)):
             copy.start()
 
     def gather_copy(b, sem, to):
@@ -169,57 +176,80 @@
         partner_blocks(s - 1)
         return carry
 
-    lax.fori_loop(1, nz, gather_step, 0)
-    partner_blocks(nz - 1)
-
-    def gather_end(zz, carry):
-        arrived(block(zz, 0, 1 - c))
-        arrived(block(zz, 1, 1 - c))
-
-        @pl.when((z < nz - 1) & (zz <= z))
-        def _():
-            up(zz).wait_send()
-
-        @pl.when((z > 0) & (zz >= z))
-        def _():
-            down(zz).wait_send()
-
-        across(zz).wait_send()
-        core(zz, 0).wait_send()
-        core(zz, 1).wait_send()
-        return carry
-
-    lax.fori_loop(0, nz, gather_end, 0)
+    lax.fori_loop(1, nz - 1, gather_step, 0)
     for j in range(1, m):
-        other = (dp + j) % m
-        for copy in weight_copies(other, other):
-            copy.wait_recv()
+        weight_copies((dp + j) % m, dp, (2,))[0].start()
+    gather_step(nz - 1, 0)
+
+    below, above = z, nz - 1 - z
+    upward = jnp.minimum(jnp.maximum(above - below, 0), 1)
+    excess = jnp.maximum(above - below, below - above)
+    paired = jnp.minimum(above, below)
+
+    def order(p):
+        inner = jnp.minimum(jnp.maximum(p - excess + 1, 0), 1)
+        q = jnp.maximum(p - excess, 0)
+        near = z + (paired - q // 2) * (1 - 2 * (q % 2)) * (2 * upward - 1)
+        far = upward * (nz - 1 - p) + (1 - upward) * p
+        return inner * near + (1 - inner) * far
 
     wide = lax.broadcasted_iota(jnp.int32, (chunk, LANES), 1)
     mine_hi = wide == me
     mine_lo = wide == me + HALF
 
-    def act_step(r, carry):
+    def chunk_weight(r):
+        weights = pay[span(r), 2 * d_all :].astype(F32)
+        return jnp.sum(jnp.where(mine_hi | mine_lo, weights, 0.0), 1, keepdims=True)
+
+    def act_step(p, carry):
+        r = order(nz - 1 - p)
+        arrived(block(r, 0, 1 - c))
+        arrived(block(r, 1, 1 - c))
         act = jnp.dot(pay[span(r), 0:d_all], gu[...], preferred_element_type=F32)
-        raw = lax.dot_general(pay[span(r), d_all : 2 * d_all], dn[...], LAST, preferred_element_type=F32)
-        weights = pay[span(r), 2 * d_all :].astype(F32)
-        w = jnp.sum(jnp.where(mine_hi | mine_lo, weights, 0.0), 1, keepdims=True)
         gate_act, up_act = act[:, 0:hid], act[:, hid:]
         sig = jax.nn.sigmoid(gate_act)
         silu = gate_act * sig
         hidden = silu * up_act
-        hw[span(r), :] = (w * hidden).astype(BF16)
-        route = jnp.sum(hidden * raw, 1, keepdims=True)
+        hh[span(r), :] = hidden.astype(BF16)
+        hw[span(r), :] = (chunk_weight(r) * hidden).astype(BF16)
+        gb[span(r), 0:hid] = (up_act * sig * (1.0 + gate_act * (1.0 - sig))).astype(BF16)
+        gb[span(r), hid:] = silu.astype(BF16)
+        return carry
+
+    for j in range(1, m):
+        other = (dp + j) % m
+        for copy in weight_copies(other, other, (0, 1)):
+            copy.wait_recv()
+    lax.fori_loop(0, nz - 1, act_step, 0)
+    partner_blocks(nz - 1)
+    act_step(nz - 1, 0)
+
+    def gather_sends(zz, carry):
+        @pl.when((z < nz - 1) & (zz <= z))
+        def _():
+            up(zz).wait_send()
+
+        @pl.when((z > 0) & (zz >= z))
+        def _():
+            down(zz).wait_send()
+
+        across(zz).wait_send()
+        core(zz, 0).wait_send()
+        core(zz, 1).wait_send()
+        return carry
+
+    def back_step(p, carry):
+        r = order(p)
+        raw = lax.dot_general(pay[span(r), d_all : 2 * d_all], dn[...], LAST, preferred_element_type=F32)
+        back = chunk_weight(r) * raw
+        route = jnp.sum(hh[span(r), :].astype(F32) * raw, 1, keepdims=True)
         route_hi = route.astype(BF16).astype(F32)
-        pay[span(r), 2 * d_all :] = jnp.where(
+        yb[span(r), 2 * d_all :] = jnp.where(
             mine_hi, route_hi, jnp.where(mine_lo, route - route_hi, 0.0)
         ).astype(BF16)
-        back = w * raw
-        gb[span(r), 0:hid] = (back * up_act * sig * (1.0 + gate_act * (1.0 - sig))).astype(BF16)
-        gb[span(r), hid:] = (back * silu).astype(BF16)
-        return carry
-
-    lax.fori_loop(0, nz, act_step, 0)
+        gb[span(r), 0:hid] = (back * gb[span(r), 0:hid].astype(F32)).astype(BF16)
+        gb[span(r), hid:] = (back * gb[span(r), hid:].astype(F32)).astype(BF16)
+        return carry
 
     piece = min(256, dl)
     pieces = dl // piece
@@ -257,56 +287,54 @@
             dstage.at[peer, i], drecv.at[owner, i], qsend_s.at[peer, i], qrecv_s.at[owner, i], dp=peer
         )
 
-    def share_step(t, carry):
+    def down_share(t, carry):
         peer = (dp + 1 + t // pieces) % m
         i = t % pieces
         dstage[peer, i] = down_part(peer, i).astype(BF16)
         down_copy(peer, dp, i).start()
+        return carry
+
+    def gate_share(t, carry):
+        peer = (dp + 1 + t // pieces) % m
+        i = t % pieces
         gstage[peer, cut(i)] = gate_part(peer, i).astype(BF16)
         gate_copy(peer, dp, i).start()
         return carry
 
-    lax.fori_loop(0, (m - 1) * pieces, share_step, 0)
-
-    def own_step(i, carry):
+    def down_own(i, carry):
         dg[0, :, cut(i)] = down_part(dp, i)
+        return carry
+
+    def gate_own(i, carry):
         own = gate_part(dp, i)
         gg[0, cut(i), :] = own[:, 0:hid]
         ug[0, cut(i), :] = own[:, hid:]
         return carry
 
-    lax.fori_loop(0, pieces, own_step, 0)
-
-    def order(p):
-        odd = p % 2
-        return (p // 2) * (1 - odd) + (nz - 1 - p // 2) * odd
-
     def core_back(d, xx):
         return remote(
-            pay.at[rows(block(d, xx, 1 - c))], crecv.at[d * 2 + xx],
+            yb.at[rows(block(d, xx, 1 - c))], crecv.at[d * 2 + xx],
             c2send_s.at[d * 2 + xx], c2recv_s.at[d * 2 + xx], expert=cp,
         )
 
     def across_back(d):
-        return remote(pay.at[rows(block(d, 1 - x, c))], xrecv.at[d], x2send_s.at[d], x2recv_s.at[d], expert=xp)
+        return remote(yb.at[rows(block(d, 1 - x, c))], xrecv.at[d], x2send_s.at[d], x2recv_s.at[d], expert=xp)
 
     def line_back(d, slot, to):
-        return remote(pay.at[rows(block(d, x, c))], zrecv.at[slot], z2send_s.at[d], z2recv_s.at[slot], expert=to)
+        return remote(yb.at[rows(block(d, x, c))], zrecv.at[slot], z2send_s.at[d], z2recv_s.at[slot], expert=to)
 
     def add(b, got):
-        pay[rows(b), :] = (pay[rows(b), :].astype(F32) + got[...].astype(F32)).astype(BF16)
+        yb[rows(b), :] = (yb[rows(b), :].astype(F32) + got[...].astype(F32)).astype(BF16)
 
     def out_step(p, carry):
         d = order(p)
-        pay[span(d), 0:d_all] = jnp.dot(hw[span(d), :], dn[...], preferred_element_type=F32).astype(BF16)
-        pay[span(d), d_all : 2 * d_all] = lax.dot_general(
+        yb[span(d), 0:d_all] = jnp.dot(hw[span(d), :], dn[...], preferred_element_type=F32).astype(BF16)
+        yb[span(d), d_all : 2 * d_all] = lax.dot_general(
             gb[span(d), :], gu[...], LAST, preferred_element_type=F32
         ).astype(BF16)
         core_back(d, 0).start()
         core_back(d, 1).start()
         return carry
-
-    lax.fori_loop(0, nz, out_step, 0)
 
     def across_step(p, carry):
         d = order(p)
@@ -317,8 +345,6 @@
         across_back(d).start()
         return carry
 
-    lax.fori_loop(0, nz, across_step, 0)
-
     def take_line(d, slot):
         line_back(d, slot, xp).wait_recv()
         add(block(d, x, c), zrecv.at[slot])
@@ -352,6 +378,39 @@
 
         return carry
 
+    lax.fori_loop(0, (m - 1) * pieces, down_share, 0)
+    for j in range(1, m):
+        other = (dp + j) % m
+        weight_copies(other, other, (2,))[0].wait_recv()
+
+    if split:
+        head = min(2, nz)
+
+        def head_step(p, carry):
+            back_step(p, carry)
+            return out_step(p, carry)
+
+        def tail_step(p, carry):
+            out_step(p, carry)
+            return across_step(p - 1, carry)
+
+        lax.fori_loop(0, head, head_step, 0)
+        lax.fori_loop(head, nz, back_step, 0)
+        lax.fori_loop(0, head - 1, across_step, 0)
+        lax.fori_loop(0, (m - 1) * pieces, gate_share, 0)
+        lax.fori_loop(head, nz, tail_step, 0)
+        across_step(nz - 1, 0)
+        lax.fori_loop(0, pieces, down_own, 0)
+        lax.fori_loop(0, pieces, gate_own, 0)
+    else:
+        lax.fori_loop(0, nz, gather_sends, 0)
+        lax.fori_loop(0, nz, back_step, 0)
+        lax.fori_loop(0, (m - 1) * pieces, gate_share, 0)
+        lax.fori_loop(0, pieces, down_own, 0)
+        lax.fori_loop(0, pieces, gate_own, 0)
+        lax.fori_loop(0, nz, out_step, 0)
+        lax.fori_loop(0, nz, across_step, 0)
+
     lax.fori_loop(0, nz, line_step, 0)
 
     @pl.when(z < nz - 1)
@@ -362,15 +421,15 @@
     def _():
         take_line(z, nz)
 
-    lo_ref[...] = pay[rows(me), 0:d_all]
-    tg_ref[...] = pay[rows(me), d_all : 2 * d_all]
-    route = pay[rows(me), 2 * d_all :].astype(F32)
+    lo_ref[...] = yb[rows(me), 0:d_all]
+    tg_ref[...] = yb[rows(me), d_all : 2 * d_all]
+    route = yb[rows(me), 2 * d_all :].astype(F32)
     slot = lax.broadcasted_iota(jnp.int32, (tb, top), 1)
     picked = jnp.zeros((tb, top), F32)
     for k in range(top):
         value = jnp.sum(jnp.where(ids[:, k : k + 1] == lane_mod, route, 0.0), 1, keepdims=True)
         picked = jnp.where(slot == k, value, picked)
-    rg_ref[...] = picked
+    rg_ref[...] = picked.T
 
     def share_end(t, carry):
         peer = (dp + 1 + t // pieces) % m
@@ -387,6 +446,8 @@
     for j in range(1, m):
         for copy in weight_copies((dp + j) % m, dp):
             copy.wait_send()
+    if split:
+        lax.fori_loop(0, nz, gather_sends, 0)
 
     def sends_end(d, carry):
         core_back(d, 0).wait_send()
@@ -400,6 +461,16 @@
         return carry
 
     lax.fori_loop(0, nz, sends_end, 0)
+
+
+def hand_over(*refs):
+    count = len(refs) // 2
+    sems = refs[-1]
+    copies = [pltpu.make_async_copy(refs[i], refs[count + i], sems.at[i]) for i in range(count)]
+    for copy in copies:
+        copy.start()
+    for copy in copies:
+        copy.wait()
 
 
 def shards(tokens, expert_ids, route_weight, out_grad, gate_weight, up_weight, down_weight):
@@ -413,13 +484,14 @@
     pieces = dl // piece
     dma = pltpu.SemaphoreType.DMA
     vmem = pl.BlockSpec(memory_space=pltpu.VMEM)
-    return tuple(
+    split = total * width * 2 <= 8 * 1024 * 1024
+    results = (
         pl.pallas_call(
-            functools.partial(kernel, n, m),
+            functools.partial(kernel, n, m, split),
             out_shape=(
                 jax.ShapeDtypeStruct((tb, d_all), BF16),
                 jax.ShapeDtypeStruct((tb, d_all), BF16),
-                jax.ShapeDtypeStruct(expert_ids.shape, F32),
+                jax.ShapeDtypeStruct(expert_ids.shape[::-1], F32),
                 jax.ShapeDtypeStruct((1, dl, hid), F32),
                 jax.ShapeDtypeStruct((1, dl, hid), F32),
                 jax.ShapeDtypeStruct((1, hid, dl), F32),
@@ -432,6 +504,7 @@
                 pltpu.VMEM((hid, d_all), BF16),
                 pltpu.VMEM((total, 2 * hid), BF16),
                 pltpu.VMEM((total, hid), BF16),
+                pltpu.VMEM((total, hid), BF16),
                 pltpu.VMEM((2 * nz, tb, width), BF16),
                 pltpu.VMEM((nz, tb, width), BF16),
                 pltpu.VMEM((nz + 1, tb, width), BF16),
@@ -442,12 +515,23 @@
                 dma((n,)), dma((nz,)), dma((nz,)), dma((nz,)), dma((2 * nz,)), dma((m, 3)), dma((m, 3)),
                 dma((m, pieces)), dma((m, pieces)), dma((m, pieces)), dma((m, pieces)),
                 dma((2 * nz,)), dma((2 * nz,)), dma((nz,)), dma((nz,)), dma((nz,)), dma((nz + 1,)),
-            ],
+            ]
+            + ([pltpu.VMEM((total, width), BF16)] if split else []),
             compiler_params=pltpu.CompilerParams(
                 collective_id=0, has_side_effects=True, vmem_limit_bytes=60 * 1024 * 1024
             ),
-        )(tokens, expert_ids, route_weight, out_grad, gate_weight, up_weight, down_weight)
+        )(tokens, expert_ids.T, route_weight.T, out_grad, gate_weight, up_weight, down_weight)
     )
+    anywhere = pl.BlockSpec(memory_space=pl.ANY)
+    layer_out, token_grad, route_grad, *grads = pl.pallas_call(
+        hand_over,
+        out_shape=tuple(jax.ShapeDtypeStruct(r.shape, r.dtype) for r in results),
+        in_specs=[anywhere] * len(results),
+        out_specs=tuple([anywhere] * len(results)),
+        scratch_shapes=[dma((len(results),))],
+        compiler_params=pltpu.CompilerParams(vmem_limit_bytes=60 * 1024 * 1024),
+    )(*results)
+    return (layer_out, token_grad, route_grad.T, *grads)
 
 
 def solution(mesh):

time: 99.2 us -> 154 us (1.55)
  the two profiles are of different devices: /device:TPU:22 before, /device:TPU:0 now
where the time goes in v2:
time: 154 us
  Pallas kernels  153 us (99%)
    pallas_call x1, Pallas kernels, shards(): pl.pallas_call(hand_over, out_shape=tuple((jax.ShapeDtypeStruct(r.shape,...  80.7 us
    pallas_call x1, Pallas kernels, shards(): pl.pallas_call(functools.partial(kernel, n, m, split), out_shape=(jax.Sha...  72.6 us

profile of v2, /device:TPU:0, one launch (start us, length us, event | category | flops | bytes accessed | tf_op | source)
XLA Modules:
  0.0 153.9 jit_solution(14350767843752385054)
XLA Ops:
  0.6 72.6 %shard_map.118 = (bf16[64,1024]{1,0:T(8,128)(2,1)}, bf16[64,1024]{1,0:T(8,128)(2,1)}, f32[8,64]{1,0:T(8,128)}, f32[1,512,384]{2,1,0:T(8,128)}, f32[1,512,384]{2,1,0:T(8,128)}, /*index=5*/f32[1,384,512]{2,1,0:T(8,128)}) custom-call(bf16[64,1024]{1,0:T(8,128)(2,1)} %tok.1, s32[8,64]{1,0:T(8,128)} %bitcast.3, f32[8,64]{1,0:T(8,128)} %bitcast.4, ...), custom_call_target="tpu_custom_call" | custom-call | tf_op jit(solution)/shard_map/pallas_call | solution.py:489
  73.2 80.7 %shard_map.119 = (bf16[64,1024]{1,0:T(8,128)(2,1)}, bf16[64,1024]{1,0:T(8,128)(2,1)}, f32[8,64]{1,0:T(8,128)}, f32[1,512,384]{2,1,0:T(8,128)}, f32[1,512,384]{2,1,0:T(8,128)}, /*index=5*/f32[1,384,512]{2,1,0:T(8,128)}) custom-call(bf16[64,1024]{1,0:T(8,128)(2,1)} %get-tuple-element.18.refs_0_, bf16[64,1024]{1,0:T(8,128)(2,1)} %get-tuple-element.19.refs_1_, ...), custom_call_target="tpu_custom_call" | custom-call | tf_op jit(solution)/shard_map/pallas_call | solution.py:526

commit v3 on v2

--- a/solution.py
+++ b/solution.py
@@ -56,6 +56,20 @@
             device_id=where, device_id_type=MESH,
         )
 
+    barrier = pltpu.get_barrier_semaphore()
+    for partner in (xp, cp):
+        pl.semaphore_signal(barrier, inc=1, device_id={"expert": partner}, device_id_type=MESH)
+
+    @pl.when(z > 0)
+    def _():
+        pl.semaphore_signal(barrier, inc=1, device_id={"expert": me - 4}, device_id_type=MESH)
+
+    @pl.when(z < nz - 1)
+    def _():
+        pl.semaphore_signal(barrier, inc=1, device_id={"expert": me + 4}, device_id_type=MESH)
+
+    for j in range(1, m):
+        pl.semaphore_signal(barrier, inc=1, device_id={"dp": (dp + j) % m}, device_id_type=MESH)
     ids = ids_t[...].T
     rw = rw_t[...].T
     lane = lax.broadcasted_iota(jnp.int32, (tb, LANES), 1)
@@ -68,20 +82,6 @@
     pay[rows(me), d_all : 2 * d_all] = og[...]
     pay[rows(me), 2 * d_all :] = jnp.where(lane < HALF, hi, dense - hi).astype(BF16)
 
-    barrier = pltpu.get_barrier_semaphore()
-    for partner in (xp, cp):
-        pl.semaphore_signal(barrier, inc=1, device_id={"expert": partner}, device_id_type=MESH)
-
-    @pl.when(z > 0)
-    def _():
-        pl.semaphore_signal(barrier, inc=1, device_id={"expert": me - 4}, device_id_type=MESH)
-
-    @pl.when(z < nz - 1)
-    def _():
-        pl.semaphore_signal(barrier, inc=1, device_id={"expert": me + 4}, device_id_type=MESH)
-
-    for j in range(1, m):
-        pl.semaphore_signal(barrier, inc=1, device_id={"dp": (dp + j) % m}, device_id_type=MESH)
     lines = jnp.minimum(z, 1) + jnp.minimum(nz - 1 - z, 1)
     pl.semaphore_wait(barrier, 1 + m + lines)
 
@@ -270,8 +270,9 @@
     def gate_part(owner, i):
         return contract(lambda at: pay[at, features(owner, i, 0)], lambda at: gb[at, :])
 
-    def down_part(owner, i):
-        return contract(lambda at: hw[at, :], lambda at: pay[at, features(owner, i, d_all)])
+    def down_part(owner):
+        mine = pl.ds(pl.multiple_of(d_all + owner * dl, dl), dl)
+        return contract(lambda at: hw[at, :], lambda at: pay[at, mine])
 
     def cut(i):
         return pl.ds(pl.multiple_of(i * piece, piece), piece)
@@ -282,16 +283,13 @@
             gsend_s.at[peer, i], grecv_s.at[owner, i], dp=peer,
         )
 
-    def down_copy(peer, owner, i):
-        return remote(
-            dstage.at[peer, i], drecv.at[owner, i], qsend_s.at[peer, i], qrecv_s.at[owner, i], dp=peer
-        )
+    def down_copy(peer, owner):
+        return remote(dstage.at[peer], drecv.at[owner], qsend_s.at[peer], qrecv_s.at[owner], dp=peer)
 
     def down_share(t, carry):
-        peer = (dp + 1 + t // pieces) % m
-        i = t % pieces
-        dstage[peer, i] = down_part(peer, i).astype(BF16)
-        down_copy(peer, dp, i).start()
+        peer = (dp + 1 + t) % m
+        dstage[peer] = down_part(peer).astype(BF16)
+        down_copy(peer, dp).start()
         return carry
 
     def gate_share(t, carry):
@@ -299,10 +297,6 @@
         i = t % pieces
         gstage[peer, cut(i)] = gate_part(peer, i).astype(BF16)
         gate_copy(peer, dp, i).start()
-        return carry
-
-    def down_own(i, carry):
-        dg[0, :, cut(i)] = down_part(dp, i)
         return carry
 
     def gate_own(i, carry):
@@ -378,13 +372,13 @@
 
         return carry
 
-    lax.fori_loop(0, (m - 1) * pieces, down_share, 0)
+    lax.fori_loop(0, m - 1, down_share, 0)
     for j in range(1, m):
         other = (dp + j) % m
         weight_copies(other, other, (2,))[0].wait_recv()
 
     if split:
-        head = min(2, nz)
+        head = 2
 
         def head_step(p, carry):
             back_step(p, carry)
@@ -395,18 +389,18 @@
             return across_step(p - 1, carry)
 
         lax.fori_loop(0, head, head_step, 0)
+        across_step(0, 0)
         lax.fori_loop(head, nz, back_step, 0)
-        lax.fori_loop(0, head - 1, across_step, 0)
         lax.fori_loop(0, (m - 1) * pieces, gate_share, 0)
         lax.fori_loop(head, nz, tail_step, 0)
         across_step(nz - 1, 0)
-        lax.fori_loop(0, pieces, down_own, 0)
+        dg[0] = down_part(dp)
         lax.fori_loop(0, pieces, gate_own, 0)
     else:
         lax.fori_loop(0, nz, gather_sends, 0)
         lax.fori_loop(0, nz, back_step, 0)
         lax.fori_loop(0, (m - 1) * pieces, gate_share, 0)
-        lax.fori_loop(0, pieces, down_own, 0)
+        dg[0] = down_part(dp)
         lax.fori_loop(0, pieces, gate_own, 0)
         lax.fori_loop(0, nz, out_step, 0)
         lax.fori_loop(0, nz, across_step, 0)
@@ -434,13 +428,18 @@
     def share_end(t, carry):
         peer = (dp + 1 + t // pieces) % m
         i = t % pieces
-        down_copy(peer, peer, i).wait()
         gate_copy(peer, peer, i).wait()
-        dg[0, :, cut(i)] += drecv[peer, i].astype(F32)
         gg[0, cut(i), :] += grecv[peer, cut(i), 0:hid].astype(F32)
         ug[0, cut(i), :] += grecv[peer, cut(i), hid:].astype(F32)
         return carry
 
+    def down_end(t, carry):
+        peer = (dp + 1 + t) % m
+        down_copy(peer, peer).wait()
+        dg[0] += drecv[peer].astype(F32)
+        return carry
+
+    lax.fori_loop(0, m - 1, down_end, 0)
     lax.fori_loop(0, (m - 1) * pieces, share_end, 0)
 
     for j in range(1, m):
@@ -463,14 +462,18 @@
     lax.fori_loop(0, nz, sends_end, 0)
 
 
-def hand_over(*refs):
-    count = len(refs) // 2
+def hand_over(count, *refs):
+    ins, outs, held = refs[:count], refs[count : 2 * count], refs[2 * count : 3 * count]
     sems = refs[-1]
-    copies = [pltpu.make_async_copy(refs[i], refs[count + i], sems.at[i]) for i in range(count)]
-    for copy in copies:
-        copy.start()
-    for copy in copies:
-        copy.wait()
+    loads = [pltpu.make_async_copy(ins[i], held[i], sems.at[0, i]) for i in range(count)]
+    stores = [pltpu.make_async_copy(held[i], outs[i], sems.at[1, i]) for i in range(count)]
+    for load in loads:
+        load.start()
+    for load, store in zip(loads, stores):
+        load.wait()
+        store.start()
+    for store in stores:
+        store.wait()
 
 
 def shards(tokens, expert_ids, route_weight, out_grad, gate_weight, up_weight, down_weight):
@@ -510,10 +513,10 @@
                 pltpu.VMEM((nz + 1, tb, width), BF16),
                 pltpu.VMEM((m, dl, 2 * hid), BF16),
                 pltpu.VMEM((m, dl, 2 * hid), BF16),
-                pltpu.VMEM((m, pieces, hid, piece), BF16),
-                pltpu.VMEM((m, pieces, hid, piece), BF16),
+                pltpu.VMEM((m, hid, dl), BF16),
+                pltpu.VMEM((m, hid, dl), BF16),
                 dma((n,)), dma((nz,)), dma((nz,)), dma((nz,)), dma((2 * nz,)), dma((m, 3)), dma((m, 3)),
-                dma((m, pieces)), dma((m, pieces)), dma((m, pieces)), dma((m, pieces)),
+                dma((m, pieces)), dma((m, pieces)), dma((m,)), dma((m,)),
                 dma((2 * nz,)), dma((2 * nz,)), dma((nz,)), dma((nz,)), dma((nz,)), dma((nz + 1,)),
             ]
             + ([pltpu.VMEM((total, width), BF16)] if split else []),
@@ -524,11 +527,11 @@
     )
     anywhere = pl.BlockSpec(memory_space=pl.ANY)
     layer_out, token_grad, route_grad, *grads = pl.pallas_call(
-        hand_over,
+        functools.partial(hand_over, len(results)),
         out_shape=tuple(jax.ShapeDtypeStruct(r.shape, r.dtype) for r in results),
         in_specs=[anywhere] * len(results),
         out_specs=tuple([anywhere] * len(results)),
-        scratch_shapes=[dma((len(results),))],
+        scratch_shapes=[pltpu.VMEM(r.shape, r.dtype) for r in results] + [dma((2, len(results)))],
         compiler_params=pltpu.CompilerParams(vmem_limit_bytes=60 * 1024 * 1024),
     )(*results)
     return (layer_out, token_grad, route_grad.T, *grads)

time: 154 us -> 75.4 us (0.49)
  Pallas kernels: 153 us -> 74.6 us
    pallas_call x1, Pallas kernels: 80.7 us -> 2.78 us  [shards(): pl.pallas_call(functools.partial(hand_over, len(results)), out_shape=tupl...]
where the time goes in v3:
time: 75.4 us; the launch traced here: 75.2 us
  Pallas kernels  74.6 us (99%)
    pallas_call x1, Pallas kernels, shards(): pl.pallas_call(functools.partial(kernel, n, m, split), out_shape=(jax.Sha...  71.8 us
    pallas_call x1, Pallas kernels, shards(): pl.pallas_call(functools.partial(hand_over, len(results)), out_shape=tupl...  2.78 us

profile of v3, /device:TPU:0, one launch (start us, length us, event | category | flops | bytes accessed | tf_op | source)
XLA Modules:
  0.0 75.2 jit_solution(4645587896211806489)
XLA Ops:
  0.6 71.8 %shard_map.118 = (bf16[64,1024]{1,0:T(8,128)(2,1)}, bf16[64,1024]{1,0:T(8,128)(2,1)}, f32[8,64]{1,0:T(8,128)}, f32[1,512,384]{2,1,0:T(8,128)}, f32[1,512,384]{2,1,0:T(8,128)}, /*index=5*/f32[1,384,512]{2,1,0:T(8,128)}) custom-call(bf16[64,1024]{1,0:T(8,128)(2,1)} %tok.1, s32[8,64]{1,0:T(8,128)} %bitcast.3, f32[8,64]{1,0:T(8,128)} %bitcast.4, ...), custom_call_target="tpu_custom_call" | custom-call | tf_op jit(solution)/shard_map/pallas_call | solution.py:492
  72.4 2.8 %shard_map.119 = (bf16[64,1024]{1,0:T(8,128)(2,1)}, bf16[64,1024]{1,0:T(8,128)(2,1)}, f32[8,64]{1,0:T(8,128)}, f32[1,512,384]{2,1,0:T(8,128)}, f32[1,512,384]{2,1,0:T(8,128)}, /*index=5*/f32[1,384,512]{2,1,0:T(8,128)}) custom-call(bf16[64,1024]{1,0:T(8,128)(2,1)} %get-tuple-element.18.refs_0_, bf16[64,1024]{1,0:T(8,128)(2,1)} %get-tuple-element.19.refs_1_, ...), custom_call_target="tpu_custom_call" | custom-call | tf_op jit(solution)/shard_map/pallas_call | solution.py:529

commit v4 on v3

--- a/solution.py
+++ b/solution.py
@@ -22,7 +22,7 @@
     lo_ref, tg_ref, rg_ref, gg, ug, dg,
     pay, gu, dn, gb, hw, hh, crecv, xrecv, zrecv, gstage, grecv, dstage, drecv,
     brecv_s, usend_s, dsend_s, xsend_s, csend_s, wsend_s, wrecv_s,
-    gsend_s, grecv_s, qsend_s, qrecv_s,
+    gsend_s, grecv_s, qsend_s, qrecv_s, local_s,
     c2send_s, c2recv_s, x2send_s, x2recv_s, z2send_s, z2recv_s,
     *sums,
 ):
@@ -70,6 +70,21 @@
 
     for j in range(1, m):
         pl.semaphore_signal(barrier, inc=1, device_id={"dp": (dp + j) % m}, device_id_type=MESH)
+    my_rows = pl.ds(pl.multiple_of(dp * dl, dl), dl)
+    local = [
+        pltpu.make_async_copy(src, dst, local_s.at[i])
+        for i, (src, dst) in enumerate(
+            (
+                (tok, pay.at[rows(me), 0:d_all]),
+                (og, pay.at[rows(me), d_all : 2 * d_all]),
+                (gw.at[0], gu.at[my_rows, 0:hid]),
+                (uw.at[0], gu.at[my_rows, hid:]),
+                (dw.at[0], dn.at[:, my_rows]),
+            )
+        )
+    ]
+    for copy in local:
+        copy.start()
     ids = ids_t[...].T
     rw = rw_t[...].T
     lane = lax.broadcasted_iota(jnp.int32, (tb, LANES), 1)
@@ -78,14 +93,10 @@
     for k in range(top):
         dense = dense + jnp.where(ids[:, k : k + 1] == lane_mod, rw[:, k : k + 1], 0.0)
     hi = dense.astype(BF16).astype(F32)
-    pay[rows(me), 0:d_all] = tok[...]
-    pay[rows(me), d_all : 2 * d_all] = og[...]
     pay[rows(me), 2 * d_all :] = jnp.where(lane < HALF, hi, dense - hi).astype(BF16)
 
     lines = jnp.minimum(z, 1) + jnp.minimum(nz - 1 - z, 1)
     pl.semaphore_wait(barrier, 1 + m + lines)
-
-    my_rows = pl.ds(pl.multiple_of(dp * dl, dl), dl)
 
     def weight_copies(peer, owner, which=(0, 1, 2)):
         own = pl.ds(pl.multiple_of(owner * dl, dl), dl)
@@ -98,80 +109,88 @@
             remote(*ends[i], wsend_s.at[peer, i], wrecv_s.at[owner, i], dp=peer) for i in which
         ]
 
+    half = tb // 2
+
+    def gather_copy(b, h, sem, to):
+        at = pl.ds(pl.multiple_of(b * tb + h * half, half), half)
+        return remote(pay.at[at], pay.at[at], sem, brecv_s.at[b, h], expert=to)
+
+    def up(zz, h):
+        return gather_copy(block(zz, x, c), h, usend_s.at[zz, h], me + 4)
+
+    def down(zz, h):
+        return gather_copy(block(zz, x, c), h, dsend_s.at[zz, h], me - 4)
+
+    def across(zz, h):
+        return gather_copy(block(zz, x, c), h, xsend_s.at[zz, h], xp)
+
+    def core(zz, xx, h):
+        return gather_copy(block(zz, xx, c), h, csend_s.at[zz * 2 + xx, h], cp)
+
+    def arrived(b, h):
+        gather_copy(b, h, xsend_s.at[0, 0], xp).wait_recv()
+
+    for copy in local[:2]:
+        copy.wait()
+    for h in range(2):
+
+        @pl.when(z < nz - 1)
+        def _():
+            up(z, h).start()
+
+        @pl.when(z > 0)
+        def _():
+            down(z, h).start()
+
+        across(z, h).start()
+        core(z, x, h).start()
     for j in range(1, m):
         for copy in weight_copies((dp + j) % m, dp, (0, 1)):
             copy.start()
 
-    def gather_copy(b, sem, to):
-        return remote(pay.at[rows(b)], pay.at[rows(b)], sem, brecv_s.at[b], expert=to)
-
-    def up(zz):
-        return gather_copy(block(zz, x, c), usend_s.at[zz], me + 4)
-
-    def down(zz):
-        return gather_copy(block(zz, x, c), dsend_s.at[zz], me - 4)
-
-    def across(zz):
-        return gather_copy(block(zz, x, c), xsend_s.at[zz], xp)
-
-    def core(zz, xx):
-        return gather_copy(block(zz, xx, c), csend_s.at[zz * 2 + xx], cp)
-
-    def arrived(b):
-        gather_copy(b, xsend_s.at[0], xp).wait_recv()
-
-    @pl.when(z < nz - 1)
-    def _():
-        up(z).start()
-
-    @pl.when(z > 0)
-    def _():
-        down(z).start()
-
-    across(z).start()
-    core(z, x).start()
-    gu[my_rows, 0:hid] = gw[0]
-    gu[my_rows, hid:] = uw[0]
-    dn[:, my_rows] = dw[0]
+    def partner_half(zz, h):
+        arrived(block(zz, 1 - x, c), h)
+        core(zz, 1 - x, h).start()
 
     def partner_blocks(s):
-        @pl.when(s == 0)
-        def _():
-            arrived(block(z, 1 - x, c))
-            core(z, 1 - x).start()
-
-        @pl.when((s > 0) & (z - s >= 0))
-        def _():
-            arrived(block(z - s, 1 - x, c))
-            core(z - s, 1 - x).start()
-
-        @pl.when((s > 0) & (z + s < nz))
-        def _():
-            arrived(block(z + s, 1 - x, c))
-            core(z + s, 1 - x).start()
+        for h in range(2):
+
+            @pl.when(s == 0)
+            def _():
+                partner_half(z, h)
+
+            @pl.when((s > 0) & (z - s >= 0))
+            def _():
+                partner_half(z - s, h)
+
+            @pl.when((s > 0) & (z + s < nz))
+            def _():
+                partner_half(z + s, h)
 
     def gather_step(s, carry):
-        @pl.when(z - s >= 0)
-        def _():
-            arrived(block(z - s, x, c))
-
-            @pl.when(z < nz - 1)
-            def _():
-                up(z - s).start()
-
-            across(z - s).start()
-            core(z - s, x).start()
-
-        @pl.when(z + s < nz)
-        def _():
-            arrived(block(z + s, x, c))
-
-            @pl.when(z > 0)
-            def _():
-                down(z + s).start()
-
-            across(z + s).start()
-            core(z + s, x).start()
+        for h in range(2):
+
+            @pl.when(z - s >= 0)
+            def _():
+                arrived(block(z - s, x, c), h)
+
+                @pl.when(z < nz - 1)
+                def _():
+                    up(z - s, h).start()
+
+                across(z - s, h).start()
+                core(z - s, x, h).start()
+
+            @pl.when(z + s < nz)
+            def _():
+                arrived(block(z + s, x, c), h)
+
+                @pl.when(z > 0)
+                def _():
+                    down(z + s, h).start()
+
+                across(z + s, h).start()
+                core(z + s, x, h).start()
 
         partner_blocks(s - 1)
         return carry
@@ -203,8 +222,9 @@
 
     def act_step(p, carry):
         r = order(nz - 1 - p)
-        arrived(block(r, 0, 1 - c))
-        arrived(block(r, 1, 1 - c))
+        for h in range(2):
+            arrived(block(r, 0, 1 - c), h)
+            arrived(block(r, 1, 1 - c), h)
         act = jnp.dot(pay[span(r), 0:d_all], gu[...], preferred_element_type=F32)
         gate_act, up_act = act[:, 0:hid], act[:, hid:]
         sig = jax.nn.sigmoid(gate_act)
@@ -216,6 +236,8 @@
         gb[span(r), hid:] = silu.astype(BF16)
         return carry
 
+    for copy in local[2:]:
+        copy.wait()
     for j in range(1, m):
         other = (dp + j) % m
         for copy in weight_copies(other, other, (0, 1)):
@@ -225,17 +247,19 @@
     act_step(nz - 1, 0)
 
     def gather_sends(zz, carry):
-        @pl.when((z < nz - 1) & (zz <= z))
-        def _():
-            up(zz).wait_send()
-
-        @pl.when((z > 0) & (zz >= z))
-        def _():
-            down(zz).wait_send()
-
-        across(zz).wait_send()
-        core(zz, 0).wait_send()
-        core(zz, 1).wait_send()
+        for h in range(2):
+
+            @pl.when((z < nz - 1) & (zz <= z))
+            def _():
+                up(zz, h).wait_send()
+
+            @pl.when((z > 0) & (zz >= z))
+            def _():
+                down(zz, h).wait_send()
+
+            across(zz, h).wait_send()
+            core(zz, 0, h).wait_send()
+            core(zz, 1, h).wait_send()
         return carry
 
     def back_step(p, carry):
@@ -372,31 +396,29 @@
 
         return carry
 
-    lax.fori_loop(0, m - 1, down_share, 0)
     for j in range(1, m):
         other = (dp + j) % m
         weight_copies(other, other, (2,))[0].wait_recv()
 
     if split:
-        head = 2
-
-        def head_step(p, carry):
-            back_step(p, carry)
-            return out_step(p, carry)
 
         def tail_step(p, carry):
             out_step(p, carry)
             return across_step(p - 1, carry)
 
-        lax.fori_loop(0, head, head_step, 0)
+        back_step(0, 0)
+        out_step(0, 0)
+        lax.fori_loop(0, m - 1, down_share, 0)
         across_step(0, 0)
-        lax.fori_loop(head, nz, back_step, 0)
+        lax.fori_loop(1, nz, back_step, 0)
+        out_step(1, 0)
         lax.fori_loop(0, (m - 1) * pieces, gate_share, 0)
-        lax.fori_loop(head, nz, tail_step, 0)
+        lax.fori_loop(2, nz, tail_step, 0)
         across_step(nz - 1, 0)
         dg[0] = down_part(dp)
         lax.fori_loop(0, pieces, gate_own, 0)
     else:
+        lax.fori_loop(0, m - 1, down_share, 0)
         lax.fori_loop(0, nz, gather_sends, 0)
         lax.fori_loop(0, nz, back_step, 0)
         lax.fori_loop(0, (m - 1) * pieces, gate_share, 0)
@@ -487,6 +509,7 @@
     pieces = dl // piece
     dma = pltpu.SemaphoreType.DMA
     vmem = pl.BlockSpec(memory_space=pltpu.VMEM)
+    anywhere = pl.BlockSpec(memory_space=pl.ANY)
     split = total * width * 2 <= 8 * 1024 * 1024
     results = (
         pl.pallas_call(
@@ -499,7 +522,7 @@
                 jax.ShapeDtypeStruct((1, dl, hid), F32),
                 jax.ShapeDtypeStruct((1, hid, dl), F32),
             ),
-            in_specs=[vmem] * 7,
+            in_specs=[anywhere, vmem, vmem] + [anywhere] * 4,
             out_specs=tuple([vmem] * 6),
             scratch_shapes=[
                 pltpu.VMEM((total, width), BF16),
@@ -515,8 +538,8 @@
                 pltpu.VMEM((m, dl, 2 * hid), BF16),
                 pltpu.VMEM((m, hid, dl), BF16),
                 pltpu.VMEM((m, hid, dl), BF16),
-                dma((n,)), dma((nz,)), dma((nz,)), dma((nz,)), dma((2 * nz,)), dma((m, 3)), dma((m, 3)),
-                dma((m, pieces)), dma((m, pieces)), dma((m,)), dma((m,)),
+                dma((n, 2)), dma((nz, 2)), dma((nz, 2)), dma((nz, 2)), dma((2 * nz, 2)), dma((m, 3)), dma((m, 3)),
+                dma((m, pieces)), dma((m, pieces)), dma((m,)), dma((m,)), dma((5,)),
                 dma((2 * nz,)), dma((2 * nz,)), dma((nz,)), dma((nz,)), dma((nz,)), dma((nz + 1,)),
             ]
             + ([pltpu.VMEM((total, width), BF16)] if split else []),
@@ -525,7 +548,6 @@
             ),
         )(tokens, expert_ids.T, route_weight.T, out_grad, gate_weight, up_weight, down_weight)
     )
-    anywhere = pl.BlockSpec(memory_space=pl.ANY)
     layer_out, token_grad, route_grad, *grads = pl.pallas_call(
         functools.partial(hand_over, len(results)),
         out_shape=tuple(jax.ShapeDtypeStruct(r.shape, r.dtype) for r in results),

time: 75.4 us -> 75.8 us (level)
  no operation moved by 1% of the time
where the time goes in v4:
time: 75.8 us; the launch traced here: 75.6 us
  Pallas kernels  75 us (99%)
    pallas_call x1, Pallas kernels, shards(): pl.pallas_call(functools.partial(kernel, n, m, split), out_shape=(jax.Sha...  72.2 us
    pallas_call x1, Pallas kernels, shards(): pl.pallas_call(functools.partial(hand_over, len(results)), out_shape=tupl...  2.78 us

profile of v4, /device:TPU:0, one launch (start us, length us, event | category | flops | bytes accessed | tf_op | source)
XLA Modules:
  0.0 75.6 jit_solution(13679320815297150031)
XLA Ops:
  0.6 72.2 %shard_map.118 = (bf16[64,1024]{1,0:T(8,128)(2,1)}, bf16[64,1024]{1,0:T(8,128)(2,1)}, f32[8,64]{1,0:T(8,128)}, f32[1,512,384]{2,1,0:T(8,128)}, f32[1,512,384]{2,1,0:T(8,128)}, /*index=5*/f32[1,384,512]{2,1,0:T(8,128)}) custom-call(bf16[64,1024]{1,0:T(8,128)(2,1)} %tok.1, s32[8,64]{1,0:T(8,128)} %bitcast.3, f32[8,64]{1,0:T(8,128)} %bitcast.4, ...), custom_call_target="tpu_custom_call" | custom-call | tf_op jit(solution)/shard_map/pallas_call | solution.py:515
  72.8 2.8 %shard_map.119 = (bf16[64,1024]{1,0:T(8,128)(2,1)}, bf16[64,1024]{1,0:T(8,128)(2,1)}, f32[8,64]{1,0:T(8,128)}, f32[1,512,384]{2,1,0:T(8,128)}, f32[1,512,384]{2,1,0:T(8,128)}, /*index=5*/f32[1,384,512]{2,1,0:T(8,128)}) custom-call(bf16[64,1024]{1,0:T(8,128)(2,1)} %get-tuple-element.18.refs_0_, bf16[64,1024]{1,0:T(8,128)(2,1)} %get-tuple-element.19.refs_1_, ...), custom_call_target="tpu_custom_call" | custom-call | tf_op jit(solution)/shard_map/pallas_call | solution.py:551

commit v5 on v4

--- a/solution.py
+++ b/solution.py
@@ -338,8 +338,14 @@
     def across_back(d):
         return remote(yb.at[rows(block(d, 1 - x, c))], xrecv.at[d], x2send_s.at[d], x2recv_s.at[d], expert=xp)
 
-    def line_back(d, slot, to):
-        return remote(yb.at[rows(block(d, x, c))], zrecv.at[slot], z2send_s.at[d], z2recv_s.at[slot], expert=to)
+    def half_rows(b, h):
+        return pl.ds(pl.multiple_of(b * tb + h * half, half), half)
+
+    def line_back(d, slot, h, to):
+        return remote(
+            yb.at[half_rows(block(d, x, c), h)], zrecv.at[slot, pl.ds(h * half, half)],
+            z2send_s.at[d, h], z2recv_s.at[slot, h], expert=to,
+        )
 
     def add(b, got):
         yb[rows(b), :] = (yb[rows(b), :].astype(F32) + got[...].astype(F32)).astype(BF16)
@@ -363,36 +369,39 @@
         across_back(d).start()
         return carry
 
-    def take_line(d, slot):
-        line_back(d, slot, xp).wait_recv()
-        add(block(d, x, c), zrecv.at[slot])
+    def take_line(d, slot, h):
+        line_back(d, slot, h, xp).wait_recv()
+        at = half_rows(block(d, x, c), h)
+        got = zrecv[slot, pl.ds(h * half, half), :]
+        yb[at, :] = (yb[at, :].astype(F32) + got.astype(F32)).astype(BF16)
 
     def line_step(p, carry):
         d = order(p)
         across_back(d).wait_recv()
         add(block(d, x, c), xrecv.at[d])
-
-        @pl.when(d < z)
-        def _():
-            @pl.when(z < nz - 1)
-            def _():
-                take_line(d, d)
-
-            line_back(d, d, me - 4).start()
-
-        @pl.when(d > z)
-        def _():
-            @pl.when(z > 0)
-            def _():
-                take_line(d, d)
-
-            @pl.when(d > z + 1)
-            def _():
-                line_back(d, d, me + 4).start()
-
-            @pl.when(d == z + 1)
-            def _():
-                line_back(d, nz, me + 4).start()
+        for h in range(2):
+
+            @pl.when(d < z)
+            def _():
+                @pl.when(z < nz - 1)
+                def _():
+                    take_line(d, d, h)
+
+                line_back(d, d, h, me - 4).start()
+
+            @pl.when(d > z)
+            def _():
+                @pl.when(z > 0)
+                def _():
+                    take_line(d, d, h)
+
+                @pl.when(d > z + 1)
+                def _():
+                    line_back(d, d, h, me + 4).start()
+
+                @pl.when(d == z + 1)
+                def _():
+                    line_back(d, nz, h, me + 4).start()
 
         return carry
 
@@ -402,21 +411,24 @@
 
     if split:
 
-        def tail_step(p, carry):
+        def more_step(p, carry):
             out_step(p, carry)
-            return across_step(p - 1, carry)
+            return across_step(p, carry)
 
         back_step(0, 0)
         out_step(0, 0)
         lax.fori_loop(0, m - 1, down_share, 0)
         across_step(0, 0)
-        lax.fori_loop(1, nz, back_step, 0)
-        out_step(1, 0)
+        back_step(1, 0)
+        more_step(1, 0)
+        lax.fori_loop(2, nz, back_step, 0)
         lax.fori_loop(0, (m - 1) * pieces, gate_share, 0)
-        lax.fori_loop(2, nz, tail_step, 0)
-        across_step(nz - 1, 0)
+        lax.fori_loop(2, nz, more_step, 0)
+        line_step(0, 0)
         dg[0] = down_part(dp)
+        line_step(1, 0)
         lax.fori_loop(0, pieces, gate_own, 0)
+        lax.fori_loop(2, nz, line_step, 0)
     else:
         lax.fori_loop(0, m - 1, down_share, 0)
         lax.fori_loop(0, nz, gather_sends, 0)
@@ -426,16 +438,17 @@
         lax.fori_loop(0, pieces, gate_own, 0)
         lax.fori_loop(0, nz, out_step, 0)
         lax.fori_loop(0, nz, across_step, 0)
-
-    lax.fori_loop(0, nz, line_step, 0)
+        lax.fori_loop(0, nz, line_step, 0)
 
     @pl.when(z < nz - 1)
     def _():
-        take_line(z, z)
+        take_line(z, z, 0)
+        take_line(z, z, 1)
 
     @pl.when(z > 0)
     def _():
-        take_line(z, nz)
+        take_line(z, nz, 0)
+        take_line(z, nz, 1)
 
     lo_ref[...] = yb[rows(me), 0:d_all]
     tg_ref[...] = yb[rows(me), d_all : 2 * d_all]
@@ -477,7 +490,8 @@
 
         @pl.when(d != z)
         def _():
-            line_back(d, d, xp).wait_send()
+            line_back(d, d, 0, xp).wait_send()
+            line_back(d, d, 1, xp).wait_send()
 
         return carry
 
@@ -540,7 +554,7 @@
                 pltpu.VMEM((m, hid, dl), BF16),
                 dma((n, 2)), dma((nz, 2)), dma((nz, 2)), dma((nz, 2)), dma((2 * nz, 2)), dma((m, 3)), dma((m, 3)),
                 dma((m, pieces)), dma((m, pieces)), dma((m,)), dma((m,)), dma((5,)),
-                dma((2 * nz,)), dma((2 * nz,)), dma((nz,)), dma((nz,)), dma((nz,)), dma((nz + 1,)),
+                dma((2 * nz,)), dma((2 * nz,)), dma((nz,)), dma((nz,)), dma((nz, 2)), dma((nz + 1, 2)),
             ]
             + ([pltpu.VMEM((total, width), BF16)] if split else []),
             compiler_params=pltpu.CompilerParams(

time: 75.8 us -> 76.1 us (level)
  no operation moved by 1% of the time
where the time goes in v5:
time: 76.1 us; the launch traced here: 75.8 us
  Pallas kernels  75.2 us (99%)
    pallas_call x1, Pallas kernels, shards(): pl.pallas_call(functools.partial(kernel, n, m, split), out_shape=(jax.Sha...  72.4 us
    pallas_call x1, Pallas kernels, shards(): pl.pallas_call(functools.partial(hand_over, len(results)), out_shape=tupl...  2.78 us

profile of v5, /device:TPU:0, one launch (start us, length us, event | category | flops | bytes accessed | tf_op | source)
XLA Modules:
  0.0 75.8 jit_solution(5797234595527644388)
XLA Ops:
  0.6 72.4 %shard_map.118 = (bf16[64,1024]{1,0:T(8,128)(2,1)}, bf16[64,1024]{1,0:T(8,128)(2,1)}, f32[8,64]{1,0:T(8,128)}, f32[1,512,384]{2,1,0:T(8,128)}, f32[1,512,384]{2,1,0:T(8,128)}, /*index=5*/f32[1,384,512]{2,1,0:T(8,128)}) custom-call(bf16[64,1024]{1,0:T(8,128)(2,1)} %tok.1, s32[8,64]{1,0:T(8,128)} %bitcast.3, f32[8,64]{1,0:T(8,128)} %bitcast.4, ...), custom_call_target="tpu_custom_call" | custom-call | tf_op jit(solution)/shard_map/pallas_call | solution.py:529
  73.1 2.8 %shard_map.119 = (bf16[64,1024]{1,0:T(8,128)(2,1)}, bf16[64,1024]{1,0:T(8,128)(2,1)}, f32[8,64]{1,0:T(8,128)}, f32[1,512,384]{2,1,0:T(8,128)}, f32[1,512,384]{2,1,0:T(8,128)}, /*index=5*/f32[1,384,512]{2,1,0:T(8,128)}) custom-call(bf16[64,1024]{1,0:T(8,128)(2,1)} %get-tuple-element.18.refs_0_, bf16[64,1024]{1,0:T(8,128)(2,1)} %get-tuple-element.19.refs_1_, ...), custom_call_target="tpu_custom_call" | custom-call | tf_op jit(solution)/shard_map/pallas_call | solution.py:565

commit v6 on v5

--- a/solution.py
+++ b/solution.py
@@ -30,6 +30,8 @@
     dl, hid = gw.shape[1], gw.shape[2]
     top = ids_t.shape[0]
     yb = sums[0] if split else pay
+    if split:
+        gu_t, dn_t, x_t, hw_t = sums[1:]
     nz = n // 4
     chunk = 4 * tb
     total = n * tb
@@ -231,7 +233,11 @@
         silu = gate_act * sig
         hidden = silu * up_act
         hh[span(r), :] = hidden.astype(BF16)
-        hw[span(r), :] = (chunk_weight(r) * hidden).astype(BF16)
+        scaled = (chunk_weight(r) * hidden).astype(BF16)
+        hw[span(r), :] = scaled
+        if split:
+            hw_t[:, span(r)] = scaled.T
+            x_t[:, span(r)] = pay[span(r), 0:d_all].T
         gb[span(r), 0:hid] = (up_act * sig * (1.0 + gate_act * (1.0 - sig))).astype(BF16)
         gb[span(r), hid:] = silu.astype(BF16)
         return carry
@@ -242,6 +248,15 @@
         other = (dp + j) % m
         for copy in weight_copies(other, other, (0, 1)):
             copy.wait_recv()
+    if split:
+
+        def turn_step(i, carry):
+            at = pl.ds(pl.multiple_of(i * 256, 256), 256)
+            gu_t[:, at] = gu[at, :].T
+            return carry
+
+        lax.fori_loop(0, d_all // 256, turn_step, 0)
+        dn_t[my_rows, :] = dn[:, my_rows].T
     lax.fori_loop(0, nz - 1, act_step, 0)
     partner_blocks(nz - 1)
     act_step(nz - 1, 0)
@@ -264,7 +279,11 @@
 
     def back_step(p, carry):
         r = order(p)
-        raw = lax.dot_general(pay[span(r), d_all : 2 * d_all], dn[...], LAST, preferred_element_type=F32)
+        grads = pay[span(r), d_all : 2 * d_all]
+        if split:
+            raw = jnp.dot(grads, dn_t[...], preferred_element_type=F32)
+        else:
+            raw = lax.dot_general(grads, dn[...], LAST, preferred_element_type=F32)
         back = chunk_weight(r) * raw
         route = jnp.sum(hh[span(r), :].astype(F32) * raw, 1, keepdims=True)
         route_hi = route.astype(BF16).astype(F32)
@@ -292,10 +311,14 @@
         return pl.ds(pl.multiple_of(shift + owner * dl + i * piece, piece), piece)
 
     def gate_part(owner, i):
+        if split:
+            return jnp.dot(x_t[features(owner, i, 0), :], gb[...], preferred_element_type=F32)
         return contract(lambda at: pay[at, features(owner, i, 0)], lambda at: gb[at, :])
 
     def down_part(owner):
         mine = pl.ds(pl.multiple_of(d_all + owner * dl, dl), dl)
+        if split:
+            return jnp.dot(hw_t[...], pay[:, mine], preferred_element_type=F32)
         return contract(lambda at: hw[at, :], lambda at: pay[at, mine])
 
     def cut(i):
@@ -353,9 +376,11 @@
     def out_step(p, carry):
         d = order(p)
         yb[span(d), 0:d_all] = jnp.dot(hw[span(d), :], dn[...], preferred_element_type=F32).astype(BF16)
-        yb[span(d), d_all : 2 * d_all] = lax.dot_general(
-            gb[span(d), :], gu[...], LAST, preferred_element_type=F32
-        ).astype(BF16)
+        if split:
+            back = jnp.dot(gb[span(d), :], gu_t[...], preferred_element_type=F32)
+        else:
+            back = lax.dot_general(gb[span(d), :], gu[...], LAST, preferred_element_type=F32)
+        yb[span(d), d_all : 2 * d_all] = back.astype(BF16)
         core_back(d, 0).start()
         core_back(d, 1).start()
         return carry
@@ -408,6 +433,9 @@
     for j in range(1, m):
         other = (dp + j) % m
         weight_copies(other, other, (2,))[0].wait_recv()
+        if split:
+            theirs = pl.ds(pl.multiple_of(other * dl, dl), dl)
+            dn_t[theirs, :] = dn[:, theirs].T
 
     if split:
 
@@ -556,7 +584,17 @@
                 dma((m, pieces)), dma((m, pieces)), dma((m,)), dma((m,)), dma((5,)),
                 dma((2 * nz,)), dma((2 * nz,)), dma((nz,)), dma((nz,)), dma((nz, 2)), dma((nz + 1, 2)),
             ]
-            + ([pltpu.VMEM((total, width), BF16)] if split else []),
+            + (
+                [
+                    pltpu.VMEM((total, width), BF16),
+                    pltpu.VMEM((2 * hid, d_all), BF16),
+                    pltpu.VMEM((d_all, hid), BF16),
+                    pltpu.VMEM((d_all, total), BF16),
+                    pltpu.VMEM((hid, total), BF16),
+                ]
+                if split
+                else []
+            ),
             compiler_params=pltpu.CompilerParams(
                 collective_id=0, has_side_effects=True, vmem_limit_bytes=60 * 1024 * 1024
             ),

time: 76.1 us -> 76 us (level)
  no operation moved by 1% of the time
where the time goes in v6:
time: 76 us; the launch traced here: 75.8 us
  Pallas kernels  75.2 us (99%)
    pallas_call x1, Pallas kernels, shards(): pl.pallas_call(functools.partial(kernel, n, m, split), out_shape=(jax.Sha...  72.4 us
    pallas_call x1, Pallas kernels, shards(): pl.pallas_call(functools.partial(hand_over, len(results)), out_shape=tupl...  2.78 us

profile of v6, /device:TPU:0, one launch (start us, length us, event | category | flops | bytes accessed | tf_op | source)
XLA Modules:
  0.0 75.8 jit_solution(2036412139385720604)
XLA Ops:
  0.6 72.4 %shard_map.118 = (bf16[64,1024]{1,0:T(8,128)(2,1)}, bf16[64,1024]{1,0:T(8,128)(2,1)}, f32[8,64]{1,0:T(8,128)}, f32[1,512,384]{2,1,0:T(8,128)}, f32[1,512,384]{2,1,0:T(8,128)}, /*index=5*/f32[1,384,512]{2,1,0:T(8,128)}) custom-call(bf16[64,1024]{1,0:T(8,128)(2,1)} %tok.1, s32[8,64]{1,0:T(8,128)} %bitcast.3, f32[8,64]{1,0:T(8,128)} %bitcast.4, ...), custom_call_target="tpu_custom_call" | custom-call | tf_op jit(solution)/shard_map/pallas_call | solution.py:557
  73.0 2.8 %shard_map.119 = (bf16[64,1024]{1,0:T(8,128)(2,1)}, bf16[64,1024]{1,0:T(8,128)(2,1)}, f32[8,64]{1,0:T(8,128)}, f32[1,512,384]{2,1,0:T(8,128)}, f32[1,512,384]{2,1,0:T(8,128)}, /*index=5*/f32[1,384,512]{2,1,0:T(8,128)}) custom-call(bf16[64,1024]{1,0:T(8,128)(2,1)} %get-tuple-element.18.refs_0_, bf16[64,1024]{1,0:T(8,128)(2,1)} %get-tuple-element.19.refs_1_, ...), custom_call_target="tpu_custom_call" | custom-call | tf_op jit(solution)/shard_map/pallas_call | solution.py:603
